TPU v7x, 32 devices: a whole 2x2x4 slice. The times are simulated.
32 devices in a mesh: dp: 4 (over z), width: 4 (over y, x), heads: 2 (over core).
Axes of the slice: x: 2, y: 2, z: 4, core: 2. Of those that a mesh axis runs over, the one named last changes fastest.
Arguments:
- inputs: bfloat16 [8192, 768], P(('dp', 'width')), may hold values from -6 to 6
- seq_lengths: int32 [4, 3], P('dp'), may hold values from 1 to 1537, 2048 in all within a row
- routes: int32 [8192, 2], P(('dp', 'width')), may hold values from 0 to 7, all different within a row; in each aligned block of 512 rows (0 to 511, 512 to 1023, ...) at most 256 rows name the same one
- norm_one: bfloat16 [768], P('width'), may hold values from 0.5 to 1.5
- qkv_weight: bfloat16 [3, 768, 768], P(None, 'width', 'heads'), may hold values from -0.21875 to 0.21875
- slopes: float32 [12], P('heads'), may hold values from 0.05 to 1
- out_weight: bfloat16 [768, 768], P('heads', 'width'), may hold values from -0.75 to 0.75
- norm_two: bfloat16 [768], P('width'), may hold values from 0.5 to 1.5
- router: bfloat16 [768, 8], P('width'), may hold values from -0.15625 to 0.15625
- expert_in: bfloat16 [8, 768, 3072], P('dp', 'width', 'heads'), may hold values from -0.21875 to 0.21875
- expert_out: bfloat16 [8, 3072, 768], P('dp', 'heads', 'width'), may hold values from -0.109375 to 0.109375
- cotangent: bfloat16 [8192, 768], P(('dp', 'width')), may hold values from -6 to 6
Outputs:
- mixed_out: bfloat16 [8192, 768], P(('dp', 'width'))
- input_grad: float32 [8192, 768], P(('dp', 'width'))
- norm_one_grad: float32 [768], P('width')
- qkv_grad: float32 [3, 768, 768], P(None, 'width', 'heads')
- slope_grad: float32 [12], P('heads')
- out_grad: float32 [768, 768], P('heads', 'width')
- norm_two_grad: float32 [768], P('width')
- router_grad: float32 [768, 8], P('width')
- expert_in_grad: float32 [8, 768, 3072], P('dp', 'width', 'heads')
- expert_out_grad: float32 [8, 3072, 768], P('dp', 'heads', 'width')
Inputs may be any that keep to these rules, and one draw needn't show every extreme that they name: `routes`: each row names two different experts. In each aligned block of 512 rows (the rows of one device), no expert is named more than 256 times, and in every draw some block names some expert exactly 256 times. `seq_lengths`: each row of 3 lengths sums to 2048, and its largest is exactly 1537.
All inputs are finite; a program needn't handle non-finite values.
Results may differ from a plain program's by a relative error of at most 0.013.
Values may be sent and summed in bfloat16 or wider, within the bound.
A program may use at most 192 MiB of HBM per device.

v0:
```python
import math

import jax
import jax.numpy as jnp
from jax import lax
from jax.sharding import PartitionSpec as P

D = 768
HD = 64


epsilon = 1e-06
highest = lax.Precision.HIGHEST


def rms_norm(values, gain_vec):
    return (
        values * lax.rsqrt(jnp.mean(values * values, axis=-1, keepdims=True) + epsilon) * gain_vec
    )


def sequence_ids(length_row, count):
    seq_ends = jnp.cumsum(length_row)
    positions = jnp.arange(count, dtype=jnp.int32)
    return jnp.sum((positions[:, None] >= seq_ends[None, :]).astype(jnp.int32), axis=1)


def pair_scores(query_blk, keys_pair, slope_pair, query_pos, seg_query, key_pos, seg_all):
    raw_scores = jnp.einsum(
        "qhd,khd->hqk", query_blk, keys_pair, preferred_element_type=jnp.float32
    ) * (1.0 / math.sqrt(HD))
    distance = jnp.maximum(query_pos[:, None] - key_pos[None, :], 0)
    decay_term = jnp.log1p(distance.astype(jnp.float32))
    allowed = (seg_query[:, None] == seg_all[None, :]) & (key_pos[None, :] <= query_pos[:, None])
    scores = jnp.where(
        allowed[None], raw_scores - slope_pair[:, None, None] * decay_term[None], -1e30
    )
    return (scores, decay_term)


def send_rows(buffer):
    return lax.all_to_all(buffer, "dp", split_axis=1, concat_axis=1, tiled=True)


def send_back(buffer):
    return lax.all_to_all(buffer, "dp", split_axis=1, concat_axis=1, tiled=True)


def shards(
    inputs,
    seq_lengths,
    routes,
    norm_one,
    qkv_weight,
    slopes,
    out_weight,
    norm_two,
    router,
    expert_in,
    expert_out,
    cotangent,
):
    w_qkv, w_proj, w_route, gain_one, gain_two, w_first, w_second = (
        lax.all_gather(qkv_weight, "width", axis=1, tiled=True),
        lax.all_gather(out_weight, "width", axis=1, tiled=True),
        lax.all_gather(router, "width", axis=0, tiled=True),
        lax.all_gather(norm_one, "width", axis=0, tiled=True),
        lax.all_gather(norm_two, "width", axis=0, tiled=True),
        lax.all_gather(expert_in, "width", axis=1, tiled=True),
        lax.all_gather(expert_out, "width", axis=2, tiled=True),
    )
    rows_own = inputs.shape[0]
    width_count = lax.axis_size("width")
    seq_total = rows_own * width_count
    row_offset = lax.axis_index("width") * rows_own
    x_vals = inputs.astype(jnp.float32)
    norm_first, back_first = jax.vjp(rms_norm, x_vals, gain_one.astype(jnp.float32))
    xn_one = norm_first.astype(jnp.bfloat16)
    qkv_vals = jnp.einsum("rd,jdc->jrc", xn_one, w_qkv, preferred_element_type=jnp.float32).astype(
        jnp.bfloat16
    )
    queries = qkv_vals[0]
    key_value = lax.all_gather(qkv_vals[1:], "width", axis=1, tiled=True)
    keys_all = key_value[0]
    values_all = key_value[1]
    seg_all = sequence_ids(seq_lengths[0], seq_total)
    key_pos = jnp.arange(seq_total, dtype=jnp.int32)
    query_pos = row_offset + jnp.arange(rows_own, dtype=jnp.int32)
    seg_query = lax.dynamic_slice_in_dim(seg_all, row_offset, rows_own, 0)
    pair_width = 2 * HD
    pair_count = queries.shape[1] // pair_width
    block_rows = min(512, rows_own)
    scale_factor = 1.0 / math.sqrt(HD)

    def pair_block(block_num, pair_num):
        row_lo = block_num * block_rows
        col_lo = pair_num * pair_width
        query_blk = queries[row_lo : row_lo + block_rows, col_lo : col_lo + pair_width].reshape(
            block_rows, 2, HD
        )
        keys_pair = keys_all[:, col_lo : col_lo + pair_width].reshape(seq_total, 2, HD)
        values_pair = values_all[:, col_lo : col_lo + pair_width].reshape(seq_total, 2, HD)
        scores, decay_term = pair_scores(
            query_blk,
            keys_pair,
            slopes[2 * pair_num : 2 * pair_num + 2],
            query_pos,
            seg_query,
            key_pos,
            seg_all,
        )
        return (query_blk, keys_pair, values_pair, scores, decay_term)

    log_sums = {}
    block_num = 0
    out_cols = []
    for pair_num in range(pair_count):
        query_blk, keys_pair, values_pair, scores, decay_term = pair_block(block_num, pair_num)
        top_score = jnp.max(scores, axis=-1, keepdims=True)
        exp_scores = jnp.exp(scores - top_score)
        row_total = jnp.sum(exp_scores, axis=-1, keepdims=True)
        log_sums[block_num, pair_num] = top_score + jnp.log(row_total)
        probs_low = (exp_scores / row_total).astype(jnp.bfloat16)
        out_cols.append(
            jnp.einsum(
                "hqk,khd->qhd", probs_low, values_pair, preferred_element_type=jnp.float32
            ).reshape(block_rows, pair_width)
        )
    out_rows = jnp.concatenate(out_cols, axis=1)
    attended = out_rows.astype(jnp.bfloat16)
    proj_part = jnp.dot(attended, w_proj, preferred_element_type=jnp.float32)
    hidden_one = x_vals + lax.psum(proj_part, "heads")
    norm_second, back_second = jax.vjp(rms_norm, hidden_one, gain_two.astype(jnp.float32))
    xn_two = norm_second.astype(jnp.bfloat16)
    logits = jnp.dot(xn_two, w_route, preferred_element_type=jnp.float32)
    chosen = jnp.take_along_axis(logits, routes, axis=1)
    gate_exp = jnp.exp(chosen - jnp.max(chosen, axis=1, keepdims=True))
    gate_vals = gate_exp / jnp.sum(gate_exp, axis=1, keepdims=True)
    expert_total = w_route.shape[1]
    local_experts = w_first.shape[0]
    data_count = lax.axis_size("dp")
    slot_cap = 4 * rows_own // expert_total
    flat_ids = routes.reshape(-1)
    expert_ids = jnp.arange(expert_total, dtype=jnp.int32)
    onehot_ids = (flat_ids[:, None] == expert_ids[None, :]).astype(jnp.int32)
    slot_rank = jnp.sum((jnp.cumsum(onehot_ids, axis=0) - onehot_ids) * onehot_ids, axis=1)
    target = (
        flat_ids % local_experts * data_count + flat_ids // local_experts
    ) * slot_cap + slot_rank
    slot_owner = (
        jnp.zeros((expert_total * slot_cap,), jnp.int32)
        .at[target]
        .set(jnp.arange(2 * rows_own, dtype=jnp.int32) + 1)
    )
    is_live = (slot_owner > 0)[:, None]
    pair_idx = jnp.maximum(slot_owner - 1, 0)
    buffer_shape = (local_experts, data_count, slot_cap, D)
    send_x = jnp.where(is_live, xn_two[pair_idx // 2], jnp.zeros((), jnp.bfloat16)).reshape(
        buffer_shape
    )
    recv_x = send_rows(send_x).reshape(local_experts, -1, D)
    expert_rows = []
    for expert_num in range(local_experts):
        pre_act = jnp.dot(
            recv_x[expert_num], w_first[expert_num], preferred_element_type=jnp.float32
        )
        activated = jax.nn.gelu(pre_act).astype(jnp.bfloat16)
        expert_rows.append(
            jnp.dot(activated, w_second[expert_num], preferred_element_type=jnp.float32).astype(
                jnp.bfloat16
            )
        )
    back_y = send_back(jnp.stack(expert_rows).reshape(buffer_shape))
    pair_y = back_y.reshape(-1, D)[target].reshape(rows_own, 2, D)
    moe_part = jnp.sum(gate_vals[:, :, None] * pair_y.astype(jnp.float32), axis=1)
    block_out = hidden_one + lax.psum(moe_part.astype(jnp.bfloat16), "heads").astype(jnp.float32)
    mixed_out = block_out.astype(jnp.bfloat16)
    grad_out = cotangent.astype(jnp.float32)
    grad_pairs = (
        (gate_vals[:, :, None] * grad_out[:, None, :]).astype(jnp.bfloat16).reshape(2 * rows_own, D)
    )
    send_grad = jnp.where(is_live, grad_pairs[pair_idx], jnp.zeros((), jnp.bfloat16)).reshape(
        buffer_shape
    )
    recv_grad = send_rows(send_grad).reshape(local_experts, -1, D)
    gate_part = jnp.sum(pair_y.astype(jnp.float32) * grad_out[:, None, :], axis=2)
    grads_first = []
    grads_second = []
    rows_back = []
    for expert_num in range(local_experts):
        rows_in = recv_x[expert_num]
        pre_act = jnp.dot(rows_in, w_first[expert_num], preferred_element_type=jnp.float32)
        activated, gelu_back = jax.vjp(jax.nn.gelu, pre_act)
        grad_rows = recv_grad[expert_num]
        grad_act = jnp.dot(grad_rows, w_second[expert_num].T, preferred_element_type=jnp.float32)
        grad_pre = gelu_back(grad_act)[0].astype(jnp.bfloat16)
        grads_second.append(
            jnp.dot(activated.astype(jnp.bfloat16).T, grad_rows, preferred_element_type=jnp.float32)
        )
        grads_first.append(jnp.dot(rows_in.T, grad_pre, preferred_element_type=jnp.float32))
        rows_back.append(
            jnp.dot(grad_pre, w_first[expert_num].T, preferred_element_type=jnp.float32).astype(
                jnp.bfloat16
            )
        )
    back_x = send_back(jnp.stack(rows_back).reshape(buffer_shape))
    grad_xn_part = jnp.sum(
        back_x.reshape(-1, D)[target].reshape(rows_own, 2, D).astype(jnp.float32), axis=1
    )
    grad_xn_two, gate_grad = lax.psum((grad_xn_part, gate_part), "heads")
    chosen_grad = gate_vals * (gate_grad - jnp.sum(gate_vals * gate_grad, axis=1, keepdims=True))
    logit_grad = jnp.sum(
        (routes[:, :, None] == expert_ids[None, None, :]).astype(jnp.float32)
        * chosen_grad[:, :, None],
        axis=1,
    )
    router_full = jnp.dot(xn_two.astype(jnp.float32).T, logit_grad, precision=highest)
    grad_xn_two = grad_xn_two + jnp.dot(
        logit_grad, w_route.astype(jnp.float32).T, precision=highest
    )
    back_hidden, gain_two_grad = back_second(grad_xn_two)
    grad_hidden = grad_out + back_hidden
    grad_branch = grad_hidden.astype(jnp.bfloat16)
    proj_grad = jnp.dot(attended.T, grad_branch, preferred_element_type=jnp.float32)
    grad_att = jnp.dot(grad_branch, w_proj.T, preferred_element_type=jnp.float32).astype(
        jnp.bfloat16
    )
    key_acc = [jnp.zeros((seq_total, 2, HD), jnp.float32) for pair_num in range(pair_count)]
    value_acc = [jnp.zeros((seq_total, 2, HD), jnp.float32) for pair_num in range(pair_count)]
    slope_acc = [jnp.zeros((2,), jnp.float32) for pair_num in range(pair_count)]
    block_num = 0
    query_cols = []
    for pair_num in range(pair_count):
        query_blk, keys_pair, values_pair, scores, decay_term = pair_block(block_num, pair_num)
        prob_vals = jnp.exp(scores - log_sums[block_num, pair_num])
        row_lo = block_num * block_rows
        col_lo = pair_num * pair_width
        grad_blk = grad_att[row_lo : row_lo + block_rows, col_lo : col_lo + pair_width].reshape(
            block_rows, 2, HD
        )
        grad_probs = jnp.einsum(
            "qhd,khd->hqk", grad_blk, values_pair, preferred_element_type=jnp.float32
        )
        grad_scores = (
            prob_vals * (grad_probs - jnp.sum(prob_vals * grad_probs, axis=-1, keepdims=True))
        ).astype(jnp.bfloat16)
        value_acc[pair_num] = jnp.einsum(
            "hqk,qhd->khd",
            prob_vals.astype(jnp.bfloat16),
            grad_blk,
            preferred_element_type=jnp.float32,
        )
        key_acc[pair_num] = (
            jnp.einsum("hqk,qhd->khd", grad_scores, query_blk, preferred_element_type=jnp.float32)
            * scale_factor
        )
        query_cols.append(
            (
                jnp.einsum(
                    "hqk,khd->qhd", grad_scores, keys_pair, preferred_element_type=jnp.float32
                )
                * scale_factor
            ).reshape(block_rows, pair_width)
        )
        slope_acc[pair_num] = slope_acc[pair_num] - jnp.sum(
            grad_scores.astype(jnp.float32) * decay_term[None], axis=(1, 2)
        )
    query_rows = jnp.concatenate(query_cols, axis=1)
    key_grad = jnp.concatenate(
        [pair_acc.reshape(seq_total, pair_width) for pair_acc in key_acc], axis=1
    )
    value_grad = jnp.concatenate(
        [pair_acc.reshape(seq_total, pair_width) for pair_acc in value_acc], axis=1
    )
    kv_grad = lax.psum_scatter(
        jnp.stack([key_grad, value_grad]), "width", scatter_dimension=1, tiled=True
    )
    qkv_cot = jnp.concatenate([query_rows[None], kv_grad], axis=0).astype(jnp.bfloat16)
    qkv_full_grad = jnp.einsum("rd,jrc->jdc", xn_one, qkv_cot, preferred_element_type=jnp.float32)
    grad_xn_part_one = jnp.einsum("jrc,jdc->rd", qkv_cot, w_qkv, preferred_element_type=jnp.float32)
    grad_xn_one = lax.psum(grad_xn_part_one, "heads")
    back_input, gain_one_grad = back_first(grad_xn_one)
    input_grad = grad_hidden + back_input
    slope_vec = jnp.concatenate(slope_acc)
    slope_tile = jnp.broadcast_to(slope_vec[None, :], (width_count, slope_vec.shape[0]))
    reduced = (
        lax.psum_scatter(qkv_full_grad, "width", scatter_dimension=1, tiled=True),
        lax.psum_scatter(proj_grad, "width", scatter_dimension=1, tiled=True),
        lax.psum_scatter(router_full, "width", scatter_dimension=0, tiled=True),
        lax.psum_scatter(gain_one_grad, "width", scatter_dimension=0, tiled=True),
        lax.psum_scatter(gain_two_grad, "width", scatter_dimension=0, tiled=True),
        lax.psum_scatter(slope_tile, "width", scatter_dimension=0, tiled=True),
        lax.psum_scatter(jnp.stack(grads_first), "width", scatter_dimension=1, tiled=True),
        lax.psum_scatter(jnp.stack(grads_second), "width", scatter_dimension=2, tiled=True),
    )
    summed = lax.psum(
        (reduced[0], reduced[1], reduced[2], reduced[3], reduced[4], reduced[5]), "dp"
    )
    return (
        mixed_out,
        input_grad,
        summed[3],
        summed[0],
        summed[5].reshape(-1),
        summed[1],
        summed[4],
        summed[2],
        reduced[6],
        reduced[7],
    )


def solution(mesh):
    return jax.shard_map(
        shards,
        mesh=mesh,
        in_specs=(
            P(("dp", "width"), None),
            P("dp", None),
            P(("dp", "width"), None),
            P("width"),
            P(None, "width", "heads"),
            P("heads"),
            P("heads", "width"),
            P("width"),
            P("width", None),
            P("dp", "width", "heads"),
            P("dp", "heads", "width"),
            P(("dp", "width"), None),
        ),
        out_specs=(
            P(("dp", "width"), None),
            P(("dp", "width"), None),
            P("width"),
            P(None, "width", "heads"),
            P("heads"),
            P("heads", "width"),
            P("width"),
            P("width", None),
            P("dp", "width", "heads"),
            P("dp", "heads", "width"),
        ),
        check_vma=False,
    )
```

profile of v0, /device:TPU:0, one launch (start us, length us, event | category | flops | bytes accessed | tf_op | source)
XLA Modules:
  0.0 1226.1 jit_solution(9754081588167594234)
XLA Ops:
  11.6 11.3 all-reduce.9
  25.0 20.2 %all-gather.6.cloned.1.call-done = bf16[3,768,384]{2,1,0:T(8,128)(2,1)} async-done(((bf16[3,192,384]{2,1,0:T(8,128)(2,1)}), bf16[3,768,384]{2,1,0:T(8,128)(2,1)}) %all-gather.6.cloned.1.call-update) | async-done | bytes 1769488 | tf_op jit(solution)/shard_map/all_gather | solution.py:64
  49.5 10.6 all_gather.27
  65.5 27.6 %all-gather.8.cloned.1.call-done = bf16[2,2048,384]{1,2,0:T(8,128)(2,1)} async-done(((bf16[2,512,384]{1,2,0:T(8,128)(2,1)}), bf16[2,2048,384]{1,2,0:T(8,128)(2,1)}) %all-gather.8.cloned.1.call-update) | async-done | bytes 3145744 | tf_op jit(solution)/shard_map/all_gather | solution.py:83
  127.2 8.1 all-gather
  154.4 6.5 gather_fusion.4
  161.7 9.4 gather_fusion
  173.2 9.4 gather_fusion.2
  192.6 68.2 %all-to-all-done.2 = bf16[2,4,256,768]{3,2,0,1:T(8,128)(2,1)S(1)} async-done(((bf16[2,4,256,768]{3,2,0,1:T(8,128)(2,1)}), bf16[2,4,256,768]{3,2,0,1:T(8,128)(2,1)S(1)}, u32[]{:S(2)}, u32[]{:S(2)}) %all-to-all-start.2) | async-done | bytes 3145760 | tf_op jit(solution)/shard_map/all_to_all | solution.py:42
  267.6 68.3 %all-to-all-done = bf16[2,4,256,768]{3,2,0,1:T(8,128)(2,1)} async-done(((bf16[2,4,256,768]{3,2,0,1:T(8,128)(2,1)}), bf16[2,4,256,768]{3,2,0,1:T(8,128)(2,1)}, u32[]{:S(2)}, u32[]{:S(2)}) %all-to-all-start) | async-done | bytes 3145760 | tf_op jit(solution)/shard_map/all_to_all | solution.py:42
  338.1 7.2 fusion.38
  345.3 8.4 fusion.19
  374.0 7.2 fusion.43
  381.3 7.2 fusion.45
  390.4 53.7 %all-to-all-done.3 = bf16[2,4,256,768]{3,2,0,1:T(8,128)(2,1)S(1)} async-done(((bf16[2,4,256,768]{3,2,0,1:T(8,128)(2,1)}), bf16[2,4,256,768]{3,2,0,1:T(8,128)(2,1)S(1)}, u32[]{:S(2)}, u32[]{:S(2)}) %all-to-all-start.3) | async-done | bytes 3145760 | tf_op jit(solution)/shard_map/all_to_all | solution.py:46
  467.8 51.2 %all-to-all-done.1 = bf16[2,4,256,768]{3,2,0,1:T(8,128)(2,1)} async-done(((bf16[2,4,256,768]{3,2,0,1:T(8,128)(2,1)}), bf16[2,4,256,768]{3,2,0,1:T(8,128)(2,1)}, u32[]{:S(2)}, u32[]{:S(2)}) %all-to-all-start.1) | async-done | bytes 3145760 | tf_op jit(solution)/shard_map/all_to_all | solution.py:46
  531.4 9.3 multiply_reduce_fusion.6
  548.6 13.5 %all-reduce.19.cloned.1.call-done = bf16[512,768]{1,0:T(8,128)(2,1)} async-done(((bf16[512,768]{1,0:T(8,128)(2,1)}), bf16[512,768]{1,0:T(8,128)(2,1)}) %all-reduce.19.cloned.1.call-update) | async-done | bytes 786448 | tf_op jit(solution)/shard_map/psum | solution.py:176
  596.2 23.3 %multiply_reduce_fusion.2 = (f32[2]{0:T(128)}, f32[2]{0:T(128)}, f32[2]{0:T(128)}, bf16[2,512,2048]{2,1,0:T(8,128)(2,1)S(1)}, bf16[2,512,2048]{2,1,0:T(8,128)(2,1)}, /*index=5*/bf16[2,512,2048]{2,1,0:T(8,128)(2,1)}) fusion(f32[512,2048]{1,0:T(8,128)} %convert_log-plus-one_fusion, f32[2,512,2048]{2,1,0:T(8,128)} %get-tuple-element.144, ...), kind=kLoop, calls=%fused_computation.14 | loop fusion | flops 44040184 | bytes 67133464 | tf_op jit(solution)/shard_map/reduce_sum | solution.py:265
  651.7 58.4 %reduce-scatter.10.cloned.1.call-done = f32[2,512,384]{2,1,0:T(8,128)} async-done(((f32[2,2048,384]{2,1,0:T(8,128)}), f32[2,512,384]{2,1,0:T(8,128)}) %reduce-scatter.10.cloned.1.call-update) | async-done | bytes 1572880 | tf_op jit(solution)/shard_map/reduce_scatter | solution.py:275
  728.3 9.2 convolution_bitcast_fusion
  737.5 8.9 convolution_bitcast_fusion.1
  748.2 8.1 pad_maximum_fusion.1
  756.3 15.0 %copy.212 = f32[2,1536,768]{1,0,2:T(2,128)} copy(f32[2,1536,768]{2,1,0:T(8,128)} %pad_maximum_fusion.1) | data formatting | bytes 18874368 | tf_op jit(solution)/shard_map/stack | solution.py:294
  779.3 26.1 %reduce-scatter.12.cloned.1.call-done = f32[384,192]{0,1:T(8,128)} async-done(((f32[384,768]{0,1:T(8,128)}), f32[384,192]{0,1:T(8,128)}) %reduce-scatter.12.cloned.1.call-update) | async-done | bytes 294928 | tf_op jit(solution)/shard_map/reduce_scatter | solution.py:288
  818.7 14.7 %reduce-scatter.18.cloned.1.call-done = f32[192,8]{1,0:T(8,128)} async-done(((f32[768,8]{1,0:T(8,128)}), f32[192,8]{1,0:T(8,128)}) %reduce-scatter.18.cloned.1.call-update) | async-done | bytes 6160
  834.6 191.4 %all-reduce.25.cloned.1.call-done = f32[2,1536,768]{1,0,2:T(2,128)} async-done(((f32[2,1536,768]{1,0,2:T(2,128)}), f32[2,1536,768]{1,0,2:T(2,128)}) %all-reduce.25.cloned.1.call-update) | async-done | bytes 9437200
  1030.2 19.1 %all-reduce.23.cloned.1.call-done = f32[512,768]{1,0:T(8,128)} async-done(((f32[512,768]{1,0:T(8,128)}), f32[512,768]{1,0:T(8,128)}) %all-reduce.23.cloned.1.call-update) | async-done | bytes 1572880 | tf_op jit(solution)/shard_map/psum | solution.py:281
  1051.4 16.2 %all-reduce.6 = (f32[768]{0:T(1024)S(1)}, f32[4,6]{1,0:T(4,128)S(1)}, f32[768]{0:T(1024)S(1)}) all-reduce(f32[768]{0:T(1024)S(1)} %get-tuple-element.87, f32[4,6]{1,0:T(4,128)S(1)} %broadcast_in_dim.78, f32[768]{0:T(1024)S(1)} %copy-done.81), channel_id=3, replica_groups=mesh['dp'=4,'width'=4,'heads'=2] {'width'}, use_global_device_ids=true, to_apply=%region_33.34.clone | all-reduce | flops 1560 | bytes 12480
  1068.4 20.5 %all-reduce.7 = (f32[192]{0:T(256)}, f32[6]{0:T(128)}, f32[192]{0:T(256)}, f32[192,8]{0,1:T(8,128)}) all-reduce(f32[192]{0:T(256)S(1)} %dynamic-slice.3, f32[6]{0:T(128)S(1)} %fusion.82, f32[192]{0:T(256)S(1)} %dynamic-slice.7, f32[192,8]{0,1:T(8,128)S(1)} %copy.219), channel_id=1, replica_groups=mesh['dp'=4,'width'=4,'heads'=2] {'dp'}, use_global_device_ids=true, to_apply=%region_34.35 | all-reduce | flops 1926 | bytes 15408 | tf_op jit(solution)/shard_map/psum | solution.py:296
  1091.9 27.8 %all-reduce.27.cloned.1.call-done = (f32[3,192,384]{1,2,0:T(8,128)}, f32[384,192]{0,1:T(8,128)}) async-done(((f32[3,192,384]{1,2,0:T(8,128)}, f32[384,192]{0,1:T(8,128)}), (f32[3,192,384]{1,2,0:T(8,128)}, f32[384,192]{0,1:T(8,128)})) %all-reduce.27.cloned.1.call-update) | async-done | bytes 1179664 | tf_op jit(solution)/shard_map/psum | solution.py:296
  1122.2 95.5 %reduce-scatter.14.cloned.1.call-done = f32[2,192,1536]{2,1,0:T(8,128)} async-done(((f32[2,768,1536]{2,1,0:T(8,128)}), f32[2,192,1536]{2,1,0:T(8,128)}) %reduce-scatter.14.cloned.1.call-update) | async-done | bytes 2359312 | tf_op jit(solution)/shard_map/reduce_scatter | solution.py:293
  (395 shorter events, 277.2 us)
Async XLA Ops:
  7.2 38.0 %all-gather.6.cloned.1.call-start = ((), (), s32[]{:S(2)}) async-start(), calls=%async_computation.9 | async-start | bytes 2211840 | tf_op jit(solution)/shard_map/all_gather | solution.py:64
  7.9 85.2 %all-gather.8.cloned.1.call-start = ((), (), s32[]{:S(2)}) async-start(), calls=%async_computation.10 | async-start | bytes 3932160 | tf_op jit(solution)/shard_map/all_gather | solution.py:83
  25.0 35.2 %copy-start.70 = (f32[512]{0:T(512)}, f32[512]{0:T(512)S(1)}, u32[]{:S(2)}) copy-start(f32[512]{0:T(512)S(1)} %fusion.80) | copy-start | bytes 6148
  25.0 35.2 %copy-start.84 = (f32[6]{0:T(128)S(1)}, f32[6]{0:T(128)}, u32[]{:S(2)}) copy-start(f32[6]{0:T(128)} %param.17) | copy-start | bytes 76
  49.1 101.9 %all-reduce.17.cloned.1.call-start = ((), (), s32[]{:S(2)}) async-start(), calls=%async_computation.11 | async-start | bytes 3145728 | tf_op jit(solution)/shard_map/psum | solution.py:132
  60.1 63.4 %copy-start.17 = (bf16[384,768]{0,1:T(8,128)(2,1)}, bf16[384,768]{0,1:T(8,128)(2,1)S(1)}, u32[]{:S(2)}) copy-start(bf16[384,768]{0,1:T(8,128)(2,1)S(1)} %all_gather.27) | copy-start | bytes 1769476
  65.4 30.4 %copy-start.32 = (bf16[512,128]{0,1:T(8,128)(2,1)}, bf16[512,128]{0,1:T(8,128)(2,1)S(1)}, u32[]{:S(2)}) copy-start(bf16[512,128]{0,1:T(8,128)(2,1)S(1)} %get-tuple-element.126) | copy-start | bytes 393220
  65.5 41.6 %copy-start.30 = (bf16[512,128]{0,1:T(8,128)(2,1)}, bf16[512,128]{0,1:T(8,128)(2,1)S(1)}, u32[]{:S(2)}) copy-start(bf16[512,128]{0,1:T(8,128)(2,1)S(1)} %get-tuple-element.125) | copy-start | bytes 393220
  65.5 49.8 %copy-start.34 = (bf16[512,128]{0,1:T(8,128)(2,1)}, bf16[512,128]{0,1:T(8,128)(2,1)S(1)}, u32[]{:S(2)}) copy-start(bf16[512,128]{0,1:T(8,128)(2,1)S(1)} %get-tuple-element.124) | copy-start | bytes 393220
  125.9 212.2 %all-gather.10.cloned.1.call-start = ((), (), s32[]{:S(2)}) async-start(), calls=%async_computation.12 | async-start | bytes 5898240 | tf_op jit(solution)/shard_map/all_gather | solution.py:69
  187.4 73.3 %all-to-all-start.2 = ((bf16[2,4,256,768]{3,2,0,1:T(8,128)(2,1)}), bf16[2,4,256,768]{3,2,0,1:T(8,128)(2,1)S(1)}, u32[]{:S(2)}, u32[]{:S(2)}) async-start(bf16[2,4,256,768]{3,2,0,1:T(8,128)(2,1)} %get-tuple-element.129), calls=%async_computation.2 | async-start | bytes 6291456 | tf_op jit(solution)/shard_map/all_to_all | solution.py:42
  192.0 153.2 %all-gather.12.cloned.1.call-start = ((), (), s32[]{:S(2)}) async-start(), calls=%async_computation.13 | async-start | bytes 5898240 | tf_op jit(solution)/shard_map/all_gather | solution.py:70
  260.8 75.2 %all-to-all-start = ((bf16[2,4,256,768]{3,2,0,1:T(8,128)(2,1)}), bf16[2,4,256,768]{3,2,0,1:T(8,128)(2,1)}, u32[]{:S(2)}, u32[]{:S(2)}) async-start(bf16[2,4,256,768]{3,2,0,1:T(8,128)(2,1)} %get-tuple-element.130), calls=%async_computation | async-start | bytes 6291456 | tf_op jit(solution)/shard_map/all_to_all | solution.py:42
  369.9 74.3 %all-to-all-start.3 = ((bf16[2,4,256,768]{3,2,0,1:T(8,128)(2,1)}), bf16[2,4,256,768]{3,2,0,1:T(8,128)(2,1)S(1)}, u32[]{:S(2)}, u32[]{:S(2)}) async-start(bf16[2,4,256,768]{3,2,0,1:T(8,128)(2,1)} %pad_maximum_fusion.4), calls=%async_computation.3 | async-start | bytes 6291456 | tf_op jit(solution)/shard_map/all_to_all | solution.py:46
  390.4 58.4 %copy-start.83 = (s32[1024,1]{0,1:T(1,128)S(1)}, s32[1024,1]{0,1:T(1,128)}, u32[]{:S(2)}) copy-start(s32[1024,1]{0,1:T(1,128)} %copy-done.82) | copy-start | bytes 12292
  444.2 74.9 %all-to-all-start.1 = ((bf16[2,4,256,768]{3,2,0,1:T(8,128)(2,1)}), bf16[2,4,256,768]{3,2,0,1:T(8,128)(2,1)}, u32[]{:S(2)}, u32[]{:S(2)}) async-start(bf16[2,4,256,768]{3,2,0,1:T(8,128)(2,1)} %pad_maximum_fusion.3), calls=%async_computation.1 | async-start | bytes 6291456 | tf_op jit(solution)/shard_map/all_to_all | solution.py:46
  448.8 95.5 %all-reduce.21.cloned.1.call-start = ((), (), s32[]{:S(2)}) async-start(), calls=%async_computation.15 | async-start | bytes 3145728 | tf_op jit(solution)/shard_map/psum | solution.py:210
  465.3 96.8 %all-reduce.19.cloned.1.call-start = ((), (), s32[]{:S(2)}) async-start(), calls=%async_computation.14 | async-start | bytes 1572864 | tf_op jit(solution)/shard_map/psum | solution.py:176
  544.2 165.9 %reduce-scatter.10.cloned.1.call-start = ((), (), s32[]{:S(2)}) async-start(), calls=%async_computation.16 | async-start | bytes 7864320 | tf_op jit(solution)/shard_map/reduce_scatter | solution.py:275
  638.6 137.7 %reduce-scatter.16.cloned.1.call-start = ((), (), s32[]{:S(2)}) async-start(), calls=%async_computation.20 | async-start | bytes 4423680
  647.0 64.6 %copy-start.11 = (bf16[512,768]{1,0:T(8,128)(2,1)S(1)}, bf16[512,768]{1,0:T(8,128)(2,1)}, u32[]{:S(2)}) copy-start(bf16[512,768]{1,0:T(8,128)(2,1)} %param.12) | copy-start | bytes 2359300
  647.0 64.6 %copy-start.64 = (f32[768]{0:T(1024)S(1)}, f32[768]{0:T(1024)}, u32[]{:S(2)}) copy-start(f32[768]{0:T(1024)} %copy-done.63) | copy-start | bytes 9220
  647.0 64.6 %copy-start.71 = (f32[512]{0:T(512)S(1)}, f32[512]{0:T(512)}, u32[]{:S(2)}) copy-start(f32[512]{0:T(512)} %copy-done.70) | copy-start | bytes 6148
  726.5 79.0 %reduce-scatter.12.cloned.1.call-start = ((), (), s32[]{:S(2)}) async-start(), calls=%async_computation.18 | async-start | bytes 1474560 | tf_op jit(solution)/shard_map/reduce_scatter | solution.py:288
  728.2 105.2 %reduce-scatter.18.cloned.1.call-start = ((), (), s32[]{:S(2)}) async-start(), calls=%async_computation.21 | async-start | bytes 491520
  748.1 277.8 %all-reduce.25.cloned.1.call-start = ((), (), s32[]{:S(2)}) async-start(), calls=%async_computation.22 | async-start | bytes 18874368
  771.4 278.0 %all-reduce.23.cloned.1.call-start = ((), (), s32[]{:S(2)}) async-start(), calls=%async_computation.17 | async-start | bytes 3145728 | tf_op jit(solution)/shard_map/psum | solution.py:281
  776.2 343.4 %all-reduce.27.cloned.1.call-start = ((), (), s32[]{:S(2)}) async-start(), calls=%async_computation.23 | async-start | bytes 2949120 | tf_op jit(solution)/shard_map/psum | solution.py:296
  805.4 412.2 %reduce-scatter.14.cloned.1.call-start = ((), (), s32[]{:S(2)}) async-start(), calls=%async_computation.19 | async-start | bytes 11796480 | tf_op jit(solution)/shard_map/reduce_scatter | solution.py:293
  834.5 214.8 %copy-start.65 = (f32[768]{0:T(1024)S(1)}, f32[768]{0:T(1024)}, u32[]{:S(2)}) copy-start(f32[768]{0:T(1024)} %copy-done.63) | copy-start | bytes 9220
  834.6 214.8 %copy-start.72 = (f32[512]{0:T(512)S(1)}, f32[512]{0:T(512)}, u32[]{:S(2)}) copy-start(f32[512]{0:T(512)} %copy-done.70) | copy-start | bytes 6148
  1028.4 60.5 %copy-start.74 = (f32[512]{0:T(512)S(1)}, f32[512]{0:T(512)}, u32[]{:S(2)}) copy-start(f32[512]{0:T(512)} %copy-done.73) | copy-start | bytes 6148
  (87 other events, 717.2 us)
Sparse Core Ops, SparseCore 0:
  9.9 35.2 all-gather.5
  49.2 43.8 all-gather.7
  126.0 20.4 all-reduce.16
  148.3 58.2 all-gather.9
  208.5 57.0 all-gather.11
  465.4 21.1 all-reduce.20
  544.4 17.6 all-reduce.18
  638.7 71.3 reduce-scatter.9
  726.6 47.2 reduce-scatter.15
  776.8 28.5 reduce-scatter.11
  809.0 24.4 reduce-scatter.17
  837.2 188.6 all-reduce.24
  1028.9 20.4 all-reduce.22
  1051.7 67.9 all-reduce.26
  1123.5 94.1 reduce-scatter.13
where the time goes:
time: 1240 us; the launch traced here: 1230 us
  waiting for transfers between devices  738 us (60%)
  matrix products  147 us (12%)
  local copies, waits for them, and re-layouts  140 us (11%)
  other arithmetic  95.4 us (8%)
  blocking collectives  69.2 us (6%)
  starting transfers between devices  19.3 us (2%)
  between operations  17.1 us (1%)
    unnamed x18, waiting for transfers between devices  208 us
    all_to_all x2, waiting for transfers between devices, send_rows(): return lax.all_to_all(buffer, 'dp', split_axis=1, concat_axis=1, tiled=True)  137 us
    all_to_all x2, waiting for transfers between devices, send_back(): return lax.all_to_all(buffer, 'dp', split_axis=1, concat_axis=1, tiled=True)  105 us
    reduce_scatter x1, waiting for transfers between devices, shards(): lax.psum_scatter(jnp.stack(grads_first), 'width', scatter_dimension=1, ti...  95.5 us
    reduce_scatter x1, waiting for transfers between devices, shards(): lax.psum_scatter(jnp.stack([key_grad, value_grad]), 'width', scatter_dime...  58.4 us
    unnamed x218, local copies, waits for them, and re-layouts  42.3 us
    psum x1, waiting for transfers between devices, shards(): lax.psum((reduced[0], reduced[1], reduced[2], reduced[3], reduced[4], red...  27.8 us
    all_gather x1, waiting for transfers between devices, shards(): key_value = lax.all_gather(qkv_vals[1:], 'width', axis=1, tiled=True)  27.6 us
  transfers between devices with their start and end apart: 19, of which 14 were waited for; matrix products, arithmetic and copies ran while one was open for 18% of the time, Pallas kernels for 0%

commit v1 on v0

v1 whole, which is shorter than its diff:
```python
import math

import jax
import jax.numpy as jnp
from jax import lax
from jax.sharding import PartitionSpec as P

D = 768
HD = 64


epsilon = 1e-06
highest = lax.Precision.HIGHEST


def rms_norm(values, gain_vec):
    return (
        values * lax.rsqrt(jnp.mean(values * values, axis=-1, keepdims=True) + epsilon) * gain_vec
    )


def pair_of(array, num):
    return array[:, 2 * HD * num : 2 * HD * (num + 1)].reshape(array.shape[0], 2, HD)


def pair_scores(query_blk, keys_pair, slope_pair, decay_term):
    raw_scores = jnp.einsum("qhd,khd->hqk", query_blk, keys_pair, preferred_element_type=jnp.float32)
    return raw_scores * (1.0 / math.sqrt(HD)) - slope_pair[:, None, None] * decay_term[None]


def pair_probs(scores):
    exp_scores = jnp.exp(scores - jnp.max(scores, axis=-1, keepdims=True))
    return exp_scores / jnp.sum(exp_scores, axis=-1, keepdims=True)


def attend(queries, keys_all, values_all, slopes, decay_term):
    out_cols = []
    for num in range(queries.shape[1] // (2 * HD)):
        scores = pair_scores(
            pair_of(queries, num), pair_of(keys_all, num), slopes[2 * num : 2 * num + 2], decay_term
        )
        out_cols.append(
            jnp.einsum(
                "hqk,khd->qhd",
                pair_probs(scores).astype(jnp.bfloat16),
                pair_of(values_all, num),
                preferred_element_type=jnp.float32,
            ).reshape(queries.shape[0], 2 * HD)
        )
    return jnp.concatenate(out_cols, axis=1).astype(jnp.bfloat16)


def attend_back(queries, keys_all, values_all, slopes, decay_term, grad_att):
    scale = 1.0 / math.sqrt(HD)
    grad_cols = ([], [], [])
    slope_cols = []

    def flat(values):
        return values.reshape(values.shape[0], 2 * HD).astype(jnp.bfloat16)

    for num in range(queries.shape[1] // (2 * HD)):
        query_blk, keys_pair, values_pair, grad_blk = [
            pair_of(array, num) for array in (queries, keys_all, values_all, grad_att)
        ]
        probs = pair_probs(
            pair_scores(query_blk, keys_pair, slopes[2 * num : 2 * num + 2], decay_term)
        )
        grad_probs = jnp.einsum(
            "qhd,khd->hqk", grad_blk, values_pair, preferred_element_type=jnp.float32
        )
        row_sum = jnp.sum(probs * grad_probs, axis=-1, keepdims=True)
        grad_scores = (probs * (grad_probs - row_sum)).astype(jnp.bfloat16)
        query_part = jnp.einsum(
            "hqk,khd->qhd", grad_scores, keys_pair, preferred_element_type=jnp.float32
        )
        key_part = jnp.einsum(
            "hqk,qhd->khd", grad_scores, query_blk, preferred_element_type=jnp.float32
        )
        value_part = jnp.einsum(
            "hqk,qhd->khd",
            probs.astype(jnp.bfloat16),
            grad_blk,
            preferred_element_type=jnp.float32,
        )
        grad_cols[0].append(flat(query_part * scale))
        grad_cols[1].append(flat(key_part * scale))
        grad_cols[2].append(flat(value_part))
        slope_cols.append(
            -jnp.sum(grad_scores.astype(jnp.float32) * decay_term[None], axis=(1, 2))
        )
    return (
        *[jnp.concatenate(cols, axis=1) for cols in grad_cols],
        jnp.concatenate(slope_cols),
    )


def swap_pairs(axis, step):
    return [(i, i ^ step) for i in range(lax.axis_size(axis))]


def hop(values, axis, step):
    return lax.ppermute(values, axis, swap_pairs(axis, step))


def pieces_of(values, axis):
    return [values] + [hop(values, axis, s) for s in range(1, lax.axis_size(axis))]


def summed_pieces(chunks, axis):
    total = chunks[0].astype(jnp.float32)
    for s in range(1, lax.axis_size(axis)):
        total = total + hop(chunks[s], axis, s).astype(jnp.float32)
    return total


def summed_everywhere(values, axis):
    step = 1
    while step < lax.axis_size(axis):
        values = values + hop(values, axis, step)
        step *= 2
    return values


def xor_columns(values, count, index):
    width = values.shape[-1] // count
    bit = 1
    while bit < count:
        blocks = [values[..., (i ^ bit) * width : ((i ^ bit) + 1) * width] for i in range(count)]
        values = jnp.where((index & bit) > 0, jnp.concatenate(blocks, axis=-1), values)
        bit *= 2
    return values


def own_half_first(values, head_index, axis):
    half = values.shape[axis] // 2
    low_half = lax.slice_in_dim(values, 0, half, axis=axis)
    high_half = lax.slice_in_dim(values, half, 2 * half, axis=axis)
    return jnp.where(head_index == 0, values, jnp.concatenate([high_half, low_half], axis=axis))


def rows_everywhere(values, half):
    found = [values]
    for s in range(1, lax.axis_size("dp")):
        piece = hop(values[:half], "dp", s)
        found.append(jnp.concatenate([piece, hop(piece, "heads", 1)], axis=0))
    return jnp.stack(found)


def rows_returned(picks, slot_rows, half):
    mine, theirs = [
        jnp.einsum("sct,scd->std", part, slot_rows, preferred_element_type=jnp.float32)
        for part in (picks[:, :, :half], picks[:, :, half:])
    ]
    theirs = hop(theirs.astype(jnp.bfloat16), "heads", 1)
    chunks = (mine + theirs.astype(jnp.float32)).astype(jnp.bfloat16)
    return summed_pieces([chunks[s] for s in range(chunks.shape[0])], "dp")


def both_halves(own, head_index):
    other = hop(own, "heads", 1)
    return jnp.where(
        head_index == 0,
        jnp.concatenate([own, other], axis=0),
        jnp.concatenate([other, own], axis=0),
    )


def beside(values):
    half = values.shape[0] // 2
    return jnp.concatenate([values[:half], values[half:]], axis=1)


def unbeside(values):
    half = values.shape[1] // 2
    return jnp.concatenate([values[:, :half], values[:, half:]], axis=0)


def shards(
    inputs,
    seq_lengths,
    routes,
    norm_one,
    qkv_weight,
    slopes,
    out_weight,
    norm_two,
    router,
    expert_in,
    expert_out,
    cotangent,
):
    rows_own = inputs.shape[0]
    half = rows_own // 2
    width_count = lax.axis_size("width")
    dp_count = lax.axis_size("dp")
    width_index = lax.axis_index("width")
    dp_index = lax.axis_index("dp")
    head_index = lax.axis_index("heads")
    expert_total = router.shape[1]
    local_experts = expert_in.shape[0]
    slot_cap = 4 * rows_own // expert_total
    block_d = norm_one.shape[0]
    heads_cols = qkv_weight.shape[2]

    small = jnp.concatenate([router.T, norm_one[None], norm_two[None]], axis=0)
    small = beside(small)
    small_rows = small.shape[0]
    pack = jnp.concatenate(
        [
            qkv_weight.reshape(3 * block_d, heads_cols),
            beside(out_weight),
            jnp.pad(small, ((0, -small_rows % 16), (0, 0))),
        ],
        axis=0,
    )
    packs = pieces_of(pack, "width")
    out_from = 3 * block_d
    small_from = out_from + out_weight.shape[0] // 2
    w_qkv = jnp.concatenate(
        [piece[:out_from].reshape(3, block_d, heads_cols) for piece in packs], axis=1
    )
    w_proj = jnp.concatenate([unbeside(piece[out_from:small_from]) for piece in packs], axis=1)
    smalls = jnp.concatenate(
        [unbeside(piece[small_from : small_from + small_rows]) for piece in packs], axis=1
    )
    w_route_t = smalls[:expert_total]
    gain_one = smalls[expert_total].astype(jnp.float32)
    gain_two = smalls[expert_total + 1].astype(jnp.float32)

    x_vals = xor_columns(inputs, width_count, width_index).astype(jnp.float32)
    cot = xor_columns(cotangent, width_count, width_index)
    grad_out = cot.astype(jnp.float32)
    norm_first, back_first = jax.vjp(rms_norm, x_vals, gain_one)
    xn_one = norm_first.astype(jnp.bfloat16)
    qkv_vals = jnp.einsum("rd,jdc->jrc", xn_one, w_qkv, preferred_element_type=jnp.float32).astype(
        jnp.bfloat16
    )
    queries = qkv_vals[0]
    kv_pieces = pieces_of(qkv_vals[1:], "width")
    expert_stack = jnp.concatenate(
        [expert_in, jnp.swapaxes(expert_out, 1, 2).astype(jnp.bfloat16)], axis=0
    )
    kv_pieces, expert_stack = lax.optimization_barrier((kv_pieces, expert_stack))
    key_value = jnp.concatenate(kv_pieces, axis=1)
    keys_all = key_value[0]
    values_all = key_value[1]
    stacks = pieces_of(expert_stack, "width")
    w_first = [
        jnp.concatenate([piece[e] for piece in stacks], axis=0) for e in range(local_experts)
    ]
    w_second_t = [
        jnp.concatenate([piece[local_experts + e] for piece in stacks], axis=0)
        for e in range(local_experts)
    ]

    cot_rows_all = rows_everywhere(own_half_first(cot, head_index, 0), half)
    routes_own = own_half_first(routes.T, head_index, 1)
    routes_all = jnp.stack(pieces_of(routes_own, "dp"))

    row_ids = jnp.arange(rows_own, dtype=jnp.int32)
    query_pos = width_index * rows_own + row_ids
    key_pos = jnp.concatenate([(width_index ^ s) * rows_own + row_ids for s in range(width_count)])
    seq_ends = jnp.cumsum(seq_lengths[0])
    seg_all = jnp.sum((key_pos[:, None] >= seq_ends[None, :]).astype(jnp.int32), axis=1)
    seg_query = seg_all[:rows_own]
    distance = jnp.maximum(query_pos[:, None] - key_pos[None, :], 0)
    allowed = (seg_query[:, None] == seg_all[None, :]) & (key_pos[None, :] <= query_pos[:, None])
    decay_term = jnp.where(allowed, jnp.log1p(distance.astype(jnp.float32)), 1e30)

    attended = attend(queries, keys_all, values_all, slopes, decay_term)
    proj_part = jnp.dot(attended, w_proj, preferred_element_type=jnp.float32)
    hidden_one = x_vals + (proj_part + hop(proj_part, "heads", 1))
    norm_second, back_second = jax.vjp(rms_norm, hidden_one, gain_two)
    xn_two = norm_second.astype(jnp.bfloat16)

    tokens = rows_everywhere(own_half_first(xn_two, head_index, 0), half)
    logits = jnp.einsum("ed,std->set", w_route_t, tokens, preferred_element_type=jnp.float32)
    expert_ids = jnp.arange(expert_total, dtype=jnp.int32)
    chosen = [
        jnp.sum(
            jnp.where(routes_all[:, k, None, :] == expert_ids[None, :, None], logits, 0.0), axis=1
        )
        for k in range(2)
    ]
    top_logit = jnp.maximum(chosen[0], chosen[1])
    gate_exp = [jnp.exp(c - top_logit) for c in chosen]
    gate_sum = gate_exp[0] + gate_exp[1]
    gates = [g / gate_sum for g in gate_exp]
    earlier = (row_ids[:, None] < row_ids[None, :]).astype(jnp.bfloat16)
    slot_ids = jnp.arange(slot_cap, dtype=jnp.int32)
    slots_picks = []
    slots_y = []
    slots_back = []
    gate_rows = []
    sums_in = []
    sums_out = []
    for e in range(local_experts):
        expert_id = dp_index * local_experts + e
        named = [routes_all[:, k] == expert_id for k in range(2)]
        member = named[0] | named[1]
        rank = jnp.dot(
            member.astype(jnp.bfloat16), earlier, preferred_element_type=jnp.float32
        ).astype(jnp.int32)
        place = jnp.where(member, rank, -1)
        picks = place[:, None, :] == slot_ids[None, :, None]
        picks_low = picks.astype(jnp.bfloat16)
        gate_token = jnp.where(named[0], gates[0], jnp.where(named[1], gates[1], 0.0))
        gate_slot = jnp.sum(jnp.where(picks, gate_token[:, None, :], 0.0), axis=2)
        rows_in = jnp.einsum(
            "sct,std->scd", picks_low, tokens, preferred_element_type=jnp.float32
        ).astype(jnp.bfloat16)
        rows_cot = jnp.einsum(
            "sct,std->scd", picks_low, cot_rows_all, preferred_element_type=jnp.float32
        )
        grad_rows = (gate_slot[:, :, None] * rows_cot).astype(jnp.bfloat16).reshape(-1, D)
        rows_in = rows_in.reshape(-1, D)
        pre_act = jnp.dot(rows_in, w_first[e], preferred_element_type=jnp.float32)
        activated, gelu_back = jax.vjp(jax.nn.gelu, pre_act)
        act_low = activated.astype(jnp.bfloat16)
        part_y = lax.dot_general(
            act_low, w_second_t[e], (((1,), (1,)), ((), ())), preferred_element_type=jnp.float32
        ).reshape(dp_count, slot_cap, D)
        gate_dot = jnp.sum(part_y * rows_cot, axis=2)
        gate_rows.append(jnp.sum(jnp.where(picks, gate_dot[:, :, None], 0.0), axis=1))
        slots_y.append((part_y * gate_slot[:, :, None]).astype(jnp.bfloat16))
        slots_picks.append(picks_low)
        grad_act = jnp.dot(grad_rows, w_second_t[e], preferred_element_type=jnp.float32)
        grad_pre = gelu_back(grad_act)[0].astype(jnp.bfloat16)
        rows_back = lax.dot_general(
            grad_pre, w_first[e], (((1,), (1,)), ((), ())), preferred_element_type=jnp.float32
        ).astype(jnp.bfloat16)
        slots_back.append(rows_back.reshape(dp_count, slot_cap, D))
        grad_second = lax.dot_general(
            grad_rows, act_low, (((0,), (0,)), ((), ())), preferred_element_type=jnp.float32
        ).astype(jnp.bfloat16)
        grad_first = lax.dot_general(
            rows_in, grad_pre, (((0,), (0,)), ((), ())), preferred_element_type=jnp.float32
        ).astype(jnp.bfloat16)
        cut = [slice(s * block_d, (s + 1) * block_d) for s in range(width_count)]
        sums_in.append(summed_pieces([grad_first[c] for c in cut], "width"))
        sums_out.append(summed_pieces([grad_second[c] for c in cut], "width"))
    expert_in_grad = jnp.stack(sums_in)
    expert_out_grad = jnp.swapaxes(jnp.stack(sums_out), 1, 2)

    all_picks = jnp.concatenate(slots_picks, axis=1)
    grad_xn_own = rows_returned(all_picks, jnp.concatenate(slots_back, axis=1), half)
    mixed_own = rows_returned(all_picks, jnp.concatenate(slots_y, axis=1), half)
    hidden_own = lax.dynamic_slice_in_dim(hidden_one, head_index * half, half, 0)
    mixed_low = (hidden_own + mixed_own).astype(jnp.bfloat16)
    mixed_out = xor_columns(both_halves(mixed_low, head_index), width_count, width_index)

    gate_parts = jnp.stack(gate_rows, axis=1)
    gate_pieces = [gate_parts[0]] + [hop(gate_parts[s], "dp", s) for s in range(1, dp_count)]
    gate_grad = []
    for k in range(2):
        found = 0.0
        for s in range(dp_count):
            for e in range(local_experts):
                match = routes_own[k] == (dp_index ^ s) * local_experts + e
                found = found + jnp.where(match, gate_pieces[s][e], 0.0)
        gate_grad.append(found)
    gate_vals = own_half_first(jnp.stack([gates[0][0], gates[1][0]]), head_index, 1)
    gate_grad = own_half_first(jnp.stack(gate_grad), head_index, 1)
    gate_grad = gate_grad + hop(gate_grad, "heads", 1)
    chosen_grad = gate_vals * (gate_grad - jnp.sum(gate_vals * gate_grad, axis=0, keepdims=True))
    logit_grad_t = jnp.sum(
        jnp.where(routes.T[:, None, :] == expert_ids[None, :, None], chosen_grad[:, None, :], 0.0),
        axis=0,
    )
    router_full_t = jnp.dot(logit_grad_t, xn_two.astype(jnp.float32), precision=highest)
    grad_xn_two = both_halves(grad_xn_own, head_index) + lax.dot_general(
        logit_grad_t,
        w_route_t.astype(jnp.float32),
        (((0,), (0,)), ((), ())),
        precision=highest,
    )
    back_hidden, gain_two_grad = back_second(grad_xn_two)
    grad_hidden = grad_out + back_hidden
    grad_branch = grad_hidden.astype(jnp.bfloat16)
    proj_grad = lax.dot_general(
        attended, grad_branch, (((0,), (0,)), ((), ())), preferred_element_type=jnp.float32
    ).astype(jnp.bfloat16)
    grad_att = lax.dot_general(
        grad_branch, w_proj, (((1,), (1,)), ((), ())), preferred_element_type=jnp.float32
    ).astype(jnp.bfloat16)
    query_grad, key_grad, value_grad, slope_grad = attend_back(
        queries, keys_all, values_all, slopes, decay_term, grad_att
    )
    kv_both = jnp.stack([key_grad, value_grad]).astype(jnp.bfloat16)
    kv_grad = summed_pieces(
        [kv_both[:, s * rows_own : (s + 1) * rows_own] for s in range(width_count)], "width"
    ).astype(jnp.bfloat16)
    qkv_cot = jnp.concatenate([query_grad[None], kv_grad], axis=0)
    grad_xn_part = jnp.einsum("jrc,jdc->rd", qkv_cot, w_qkv, preferred_element_type=jnp.float32)
    grad_xn_one = grad_xn_part + hop(grad_xn_part, "heads", 1)
    qkv_full_grad = jnp.einsum(
        "rd,jrc->jdc", xn_one, qkv_cot, preferred_element_type=jnp.float32
    ).astype(jnp.bfloat16)
    back_input, gain_one_grad = back_first(grad_xn_one)
    input_grad = xor_columns(grad_hidden + back_input, width_count, width_index)

    grad_chunks = [
        jnp.concatenate(
            [
                qkv_full_grad[:, c].reshape(3 * block_d, heads_cols),
                beside(proj_grad[:, c]),
            ],
            axis=0,
        )
        for c in cut
    ]
    own_grads = summed_pieces(grad_chunks, "width").astype(jnp.bfloat16)
    part_rows = own_grads.shape[0] // dp_count

    def part_of(s):
        return lax.dynamic_slice_in_dim(own_grads, (dp_index ^ s) * part_rows, part_rows, 0)

    grad_part = summed_pieces([part_of(s) for s in range(dp_count)], "dp").astype(jnp.bfloat16)
    grads = jnp.zeros_like(own_grads)
    for s, piece in enumerate(pieces_of(grad_part, "dp")):
        grads = lax.dynamic_update_slice_in_dim(grads, piece, (dp_index ^ s) * part_rows, 0)
    grads = grads.astype(jnp.float32)
    qkv_grad = grads[:out_from].reshape(3, block_d, heads_cols)
    out_grad = unbeside(grads[out_from:])

    tiny = jnp.concatenate([router_full_t, gain_one_grad[None], gain_two_grad[None]], axis=0)
    slope_row = jnp.pad(slope_grad, (0, block_d - slope_grad.shape[0]))[None]
    tiny_sum = summed_pieces([jnp.concatenate([tiny[:, c], slope_row], axis=0) for c in cut], "width")
    tiny_sum = summed_everywhere(tiny_sum, "dp")
    return (
        mixed_out,
        input_grad,
        tiny_sum[expert_total],
        qkv_grad,
        tiny_sum[expert_total + 2, : slope_grad.shape[0]],
        out_grad,
        tiny_sum[expert_total + 1],
        tiny_sum[:expert_total].T,
        expert_in_grad,
        expert_out_grad,
    )


def solution(mesh):
    return jax.shard_map(
        shards,
        mesh=mesh,
        in_specs=(
            P(("dp", "width"), None),
            P("dp", None),
            P(("dp", "width"), None),
            P("width"),
            P(None, "width", "heads"),
            P("heads"),
            P("heads", "width"),
            P("width"),
            P("width", None),
            P("dp", "width", "heads"),
            P("dp", "heads", "width"),
            P(("dp", "width"), None),
        ),
        out_specs=(
            P(("dp", "width"), None),
            P(("dp", "width"), None),
            P("width"),
            P(None, "width", "heads"),
            P("heads"),
            P("heads", "width"),
            P("width"),
            P("width", None),
            P("dp", "width", "heads"),
            P("dp", "heads", "width"),
        ),
        check_vma=False,
    )
```

time: 1240 us -> 697 us (0.56)
  waiting for transfers between devices: 738 us -> 314 us
  local copies, waits for them, and re-layouts: 140 us -> 58.9 us
  blocking collectives: 69.2 us -> 0 us
  starting transfers between devices: 19.3 us -> 80.7 us
  other arithmetic: 95.4 us -> 71 us
  between operations: 17.1 us -> 3.09 us
    ppermute x0 -> x69, waiting for transfers between devices: none -> 314 us  [hop(): return lax.ppermute(values, axis, swap_pairs(axis, step))]
    all_to_all x4 -> x0, waiting for transfers between devices: 241 us -> none  [the longest x2 137 us: send_rows(): return lax.all_to_all(buffer, 'dp', split_axis=1, concat_axis=1, tiled=True)]
    unnamed x18 -> x0, waiting for transfers between devices: 208 us -> none
    reduce_scatter x3 -> x0, waiting for transfers between devices: 180 us -> none  [the longest x1 95.5 us: shards(): lax.psum_scatter(jnp.stack(grads_first), 'width', scatter_dimension=1, ti...]
    ppermute x0 -> x69, starting transfers between devices: none -> 80.7 us  [hop(): return lax.ppermute(values, axis, swap_pairs(axis, step))]
    psum x5 -> x0, waiting for transfers between devices: 60.4 us -> none  [the longest x1 27.8 us: shards(): lax.psum((reduced[0], reduced[1], reduced[2], reduced[3], reduced[4], red...]
    all_gather x4 -> x0, waiting for transfers between devices: 47.9 us -> none  [the longest x1 27.6 us: shards(): key_value = lax.all_gather(qkv_vals[1:], 'width', axis=1, tiled=True)]
    gather x9 -> x0, local copies, waits for them, and re-layouts: 36.6 us -> none  [the longest x1 9.42 us: shards(): xn_two[pair_idx // 2]]
  transfers between devices with their start and end apart: 19 -> 69, of which waited for: 14 -> 36; matrix products, arithmetic and copies ran while one was open for 18% -> 21% of each run, Pallas kernels for 0% -> 0%
where the time goes in v1:
time: 697 us; the launch traced here: 687 us
  waiting for transfers between devices  314 us (45%)
  matrix products  159 us (23%)
  starting transfers between devices  80.7 us (12%)
  other arithmetic  71 us (10%)
  local copies, waits for them, and re-layouts  58.9 us (8%)
    ppermute x69, waiting for transfers between devices, hop(): return lax.ppermute(values, axis, swap_pairs(axis, step))  314 us
    ppermute x69, starting transfers between devices, hop(): return lax.ppermute(values, axis, swap_pairs(axis, step))  80.7 us
    sub x3, matrix products, pair_probs(): exp_scores = jnp.exp(scores - jnp.max(scores, axis=-1, keepdims=True))  27.1 us
    reduce_sum x1, other arithmetic, attend_back(): jnp.sum(grad_scores.astype(jnp.float32) * decay_term[None], axis=(1, 2))  20.6 us
    dot_general x2, matrix products, shards(): jnp.dot(grad_rows, w_second_t[e], preferred_element_type=jnp.float32)  15.7 us
    dot_general x3, matrix products, attend(): jnp.einsum('hqk,khd->qhd', pair_probs(scores).astype(jnp.bfloat16), pair_...  14.9 us
  transfers between devices with their start and end apart: 69, of which 36 were waited for; matrix products, arithmetic and copies ran while one was open for 21% of the time, Pallas kernels for 0%

profile of v1, /device:TPU:0, one launch (start us, length us, event | category | flops | bytes accessed | tf_op | source)
XLA Modules:
  0.0 687.0 jit_solution(5208945024741484256)
XLA Ops:
  2.1 5.0 collective-permute-start.9
  64.6 12.7 %collective-permute-done.5 = bf16[2,512,384]{1,2,0:T(8,128)(2,1)S(1)} collective-permute-done((bf16[2,512,384]{1,2,0:T(8,128)(2,1)S(1)}, bf16[2,512,384]{1,2,0:T(8,128)(2,1)S(1)}, u32[]{:S(2)}, u32[]{:S(2)}) %collective-permute-start.5) | collective-permute-done | bytes 786464 | tf_op jit(solution)/shard_map/ppermute | solution.py:102
  78.7 14.5 %collective-permute-done.4 = bf16[2,512,384]{1,2,0:T(8,128)(2,1)S(1)} collective-permute-done((bf16[2,512,384]{1,2,0:T(8,128)(2,1)S(1)}, bf16[2,512,384]{1,2,0:T(8,128)(2,1)S(1)}, u32[]{:S(2)}, u32[]{:S(2)}) %collective-permute-start.4) | collective-permute-done | bytes 786464 | tf_op jit(solution)/shard_map/ppermute | solution.py:102
  95.8 9.1 %fusion.224 = (f32[2,512]{1,0:T(2,128)}, f32[2,512,2048]{2,1,0:T(8,128)}) fusion(f32[512,2048]{1,0:T(8,128)} %log-plus-one_select_fusion, f32[2]{0:T(128)} %get-tuple-element.219, bf16[512,2,64]{0,2,1:T(8,128)(2,1)S(1)} %bitcast.355, bf16[2048,2,64]{0,2,1:T(8,128)(2,1)} %bitcast.331), kind=kOutput, calls=%fused_computation.457 | convolution fusion | flops 278923264 | bytes 13242376 | tf_op jit(solution)/shard_map/sub | solution.py:32
  104.9 5.0 fusion.67
  110.0 8.9 %fusion.223 = (f32[2,512]{1,0:T(2,128)}, f32[2,512,2048]{2,1,0:T(8,128)}) fusion(f32[2]{0:T(128)} %get-tuple-element.221, f32[512,2048]{1,0:T(8,128)} %log-plus-one_select_fusion, bf16[512,2,64]{0,2,1:T(8,128)(2,1)S(1)} %bitcast.359, bf16[2048,2,64]{0,2,1:T(8,128)(2,1)} %bitcast.335), kind=kOutput, calls=%fused_computation.456 | convolution fusion | flops 278923264 | bytes 13242376 | tf_op jit(solution)/shard_map/sub | solution.py:32
  123.8 9.0 %fusion.222 = (f32[2,512]{1,0:T(2,128)}, f32[2,512,2048]{2,1,0:T(8,128)}) fusion(f32[2]{0:T(128)} %get-tuple-element.220, f32[512,2048]{1,0:T(8,128)} %log-plus-one_select_fusion, bf16[512,2,64]{0,2,1:T(8,128)(2,1)S(1)} %bitcast.357, bf16[2048,2,64]{0,2,1:T(8,128)(2,1)} %bitcast.333), kind=kOutput, calls=%fused_computation.455 | convolution fusion | flops 278923264 | bytes 13242376 | tf_op jit(solution)/shard_map/sub | solution.py:32
  156.4 6.5 collective-permute-done.14
  162.9 23.4 %collective-permute-done.12 = bf16[256,768]{1,0:T(8,128)(2,1)S(1)} collective-permute-done((bf16[256,768]{1,0:T(8,128)(2,1)S(1)}, bf16[256,768]{1,0:T(8,128)(2,1)S(1)}, u32[]{:S(2)}, u32[]{:S(2)}) %collective-permute-start.12) | collective-permute-done | bytes 393248 | tf_op jit(solution)/shard_map/ppermute | solution.py:102
  197.0 13.1 %collective-permute-done.18 = bf16[4,192,1536]{2,1,0:T(8,128)(2,1)S(1)} collective-permute-done((bf16[4,192,1536]{2,1,0:T(8,128)(2,1)S(1)}, bf16[4,192,1536]{2,1,0:T(8,128)(2,1)S(1)}, u32[]{:S(2)}, u32[]{:S(2)}) %collective-permute-start.18) | collective-permute-done | bytes 2359328 | tf_op jit(solution)/shard_map/ppermute | solution.py:102
  210.3 48.6 %collective-permute-done.17 = bf16[4,192,1536]{2,1,0:T(8,128)(2,1)S(1)} collective-permute-done((bf16[4,192,1536]{2,1,0:T(8,128)(2,1)S(1)}, bf16[4,192,1536]{2,1,0:T(8,128)(2,1)S(1)}, u32[]{:S(2)}, u32[]{:S(2)}) %collective-permute-start.17) | collective-permute-done | bytes 2359328 | tf_op jit(solution)/shard_map/ppermute | solution.py:102
  263.9 6.5 fusion.101
  272.3 7.8 %fusion.16 = bf16[1024,1536]{1,0:T(8,128)(2,1)S(1)} fusion(f32[1024,1536]{1,0:T(8,128)} %fusion.102, bf16[1024,768]{1,0:T(8,128)(2,1)S(1)} %bitcast.350, bf16[192,1536]{1,0:T(8,128)(2,1)S(1)} %get-tuple-element.109, bf16[192,1536]{1,0:T(8,128)(2,1)S(1)} %get-tuple-element.105, bf16[192,1536]{1,0:T(8,128)(2,1)S(1)} %get-tuple-element.101, ...), kind=kOutput, calls=%fused_computation.35 | convolution fusion | flops 2456813568 | bytes 13369344 | tf_op jit(solution)/shard_map/dot_general | solution.py:327
  280.1 5.7 convolution_convert_fusion
  296.2 6.5 fusion.104
  304.6 7.8 %fusion.9 = bf16[1024,1536]{1,0:T(8,128)(2,1)S(1)} fusion(f32[1024,1536]{1,0:T(8,128)} %fusion.105, bf16[1024,768]{1,0:T(8,128)(2,1)S(1)} %bitcast.352, bf16[192,1536]{1,0:T(8,128)(2,1)S(1)} %get-tuple-element.111, bf16[192,1536]{1,0:T(8,128)(2,1)S(1)} %get-tuple-element.107, bf16[192,1536]{1,0:T(8,128)(2,1)S(1)} %get-tuple-element.103, ...), kind=kOutput, calls=%fused_computation.28 | convolution fusion | flops 2456813568 | bytes 13369344 | tf_op jit(solution)/shard_map/dot_general | solution.py:327
  312.4 5.7 convolution_convert_fusion.1
  343.0 11.1 %collective-permute-done.62 = bf16[192,1536]{1,0:T(8,128)(2,1)S(1)} collective-permute-done((bf16[192,1536]{1,0:T(8,128)(2,1)S(1)}, bf16[192,1536]{1,0:T(8,128)(2,1)S(1)}, u32[]{:S(2)}, u32[]{:S(2)}) %collective-permute-start.62) | collective-permute-done | bytes 589856 | tf_op jit(solution)/shard_map/ppermute | solution.py:102
  354.1 9.1 %collective-permute-done.61 = bf16[192,1536]{1,0:T(8,128)(2,1)S(1)} collective-permute-done((bf16[192,1536]{1,0:T(8,128)(2,1)S(1)}, bf16[192,1536]{1,0:T(8,128)(2,1)S(1)}, u32[]{:S(2)}, u32[]{:S(2)}) %collective-permute-start.61) | collective-permute-done | bytes 589856 | tf_op jit(solution)/shard_map/ppermute | solution.py:102
  367.3 12.1 %collective-permute-done.68 = bf16[192,1536]{1,0:T(8,128)(2,1)S(1)} collective-permute-done((bf16[192,1536]{1,0:T(8,128)(2,1)S(1)}, bf16[192,1536]{1,0:T(8,128)(2,1)S(1)}, u32[]{:S(2)}, u32[]{:S(2)}) %collective-permute-start.68) | collective-permute-done | bytes 589856 | tf_op jit(solution)/shard_map/ppermute | solution.py:102
  380.3 8.2 %collective-permute-done.67 = bf16[192,1536]{1,0:T(8,128)(2,1)S(1)} collective-permute-done((bf16[192,1536]{1,0:T(8,128)(2,1)S(1)}, bf16[192,1536]{1,0:T(8,128)(2,1)S(1)}, u32[]{:S(2)}, u32[]{:S(2)}) %collective-permute-start.67) | collective-permute-done | bytes 589856 | tf_op jit(solution)/shard_map/ppermute | solution.py:102
  392.6 12.1 %collective-permute-done.59 = bf16[192,1536]{1,0:T(8,128)(2,1)S(1)} collective-permute-done((bf16[192,1536]{1,0:T(8,128)(2,1)S(1)}, bf16[192,1536]{1,0:T(8,128)(2,1)S(1)}, u32[]{:S(2)}, u32[]{:S(2)}) %collective-permute-start.59) | collective-permute-done | bytes 589856 | tf_op jit(solution)/shard_map/ppermute | solution.py:102
  406.2 5.1 collective-permute-done.58
  420.6 8.5 %collective-permute-done.65 = bf16[192,1536]{1,0:T(8,128)(2,1)S(1)} collective-permute-done((bf16[192,1536]{1,0:T(8,128)(2,1)S(1)}, bf16[192,1536]{1,0:T(8,128)(2,1)S(1)}, u32[]{:S(2)}, u32[]{:S(2)}) %collective-permute-start.65) | collective-permute-done | bytes 589856 | tf_op jit(solution)/shard_map/ppermute | solution.py:102
  431.5 5.4 collective-permute-done.64
  440.6 20.2 %collective-permute-done.33 = bf16[256,768]{1,0:T(8,128)(2,1)S(1)} collective-permute-done((bf16[256,768]{1,0:T(8,128)(2,1)S(1)}, bf16[256,768]{1,0:T(8,128)(2,1)S(1)}, u32[]{:S(2)}, u32[]{:S(2)}) %collective-permute-start.33) | collective-permute-done | bytes 393248 | tf_op jit(solution)/shard_map/ppermute | solution.py:102
  460.8 28.6 %collective-permute-done.32 = bf16[256,768]{1,0:T(8,128)(2,1)S(1)} collective-permute-done((bf16[256,768]{1,0:T(8,128)(2,1)S(1)}, bf16[256,768]{1,0:T(8,128)(2,1)S(1)}, u32[]{:S(2)}, u32[]{:S(2)}) %collective-permute-start.32) | collective-permute-done | bytes 393248 | tf_op jit(solution)/shard_map/ppermute | solution.py:102
  516.5 20.6 %multiply_reduce_fusion.2 = (f32[2]{0:T(128)}, f32[2]{0:T(128)}, f32[2]{0:T(128)S(1)}, bf16[2,512,2048]{2,1,0:T(8,128)(2,1)}, bf16[2,512,2048]{2,1,0:T(8,128)(2,1)S(1)}, /*index=5*/bf16[2,512,2048]{2,1,0:T(8,128)(2,1)S(1)}) fusion(f32[512,2048]{1,0:T(8,128)S(1)} %copy-done.1, f32[2,512,2048]{2,1,0:T(8,128)} %get-tuple-element.230, ...), kind=kLoop, calls=%fused_computation.9 | loop fusion | flops 44040184 | bytes 67133464 | tf_op jit(solution)/shard_map/reduce_sum | solution.py:89
  567.6 11.1 %collective-permute-done.39 = bf16[2,512,384]{2,1,0:T(8,128)(2,1)} collective-permute-done((bf16[2,512,384]{2,1,0:T(8,128)(2,1)}, bf16[2,512,384]{2,1,0:T(8,128)(2,1)}, u32[]{:S(2)}, u32[]{:S(2)}) %collective-permute-start.39) | collective-permute-done | bytes 786464 | tf_op jit(solution)/shard_map/ppermute | solution.py:102
  578.7 16.5 %collective-permute-done.41 = bf16[2,512,384]{2,1,0:T(8,128)(2,1)} collective-permute-done((bf16[2,512,384]{2,1,0:T(8,128)(2,1)}, bf16[2,512,384]{2,1,0:T(8,128)(2,1)}, u32[]{:S(2)}, u32[]{:S(2)}) %collective-permute-start.41) | collective-permute-done | bytes 786464 | tf_op jit(solution)/shard_map/ppermute | solution.py:102
  623.7 12.2 %collective-permute-done.49 = bf16[768,384]{1,0:T(8,128)(2,1)} collective-permute-done((bf16[768,384]{1,0:T(8,128)(2,1)}, bf16[768,384]{1,0:T(8,128)(2,1)}, u32[]{:S(2)}, u32[]{:S(2)}) %collective-permute-start.49) | collective-permute-done | bytes 589856 | tf_op jit(solution)/shard_map/ppermute | solution.py:102
  645.9 8.1 %collective-permute-done.52 = bf16[192,384]{1,0:T(8,128)(2,1)S(1)} collective-permute-done((bf16[192,384]{1,0:T(8,128)(2,1)S(1)}, bf16[192,384]{1,0:T(8,128)(2,1)S(1)}, u32[]{:S(2)}, u32[]{:S(2)}) %collective-permute-start.52) | collective-permute-done | bytes 147488 | tf_op jit(solution)/shard_map/ppermute | solution.py:102
  (546 shorter events, 299.1 us)
Async XLA Ops:
  2.1 28.8 %collective-permute-start.9 = (s32[2,512]{1,0:T(2,128)S(1)}, s32[2,512]{1,0:T(2,128)S(1)}, u32[]{:S(2)}, u32[]{:S(2)}) collective-permute-start(s32[2,512]{1,0:T(2,128)S(1)} %add_select_fusion), channel_id=1, source_target_pairs={{0,24},{8,16},{16,8},{24,0},{1,25},{9,17},{17,9},{25,1},{2,26},{10... | collective-permute-start | bytes 12296 | tf_op jit(solution)/shard_map/ppermute | solution.py:102
  7.2 27.9 %collective-permute-start.7 = (s32[2,512]{1,0:T(2,128)S(1)}, s32[2,512]{1,0:T(2,128)S(1)}, u32[]{:S(2)}, u32[]{:S(2)}) collective-permute-start(s32[2,512]{1,0:T(2,128)S(1)} %add_select_fusion), channel_id=1, source_target_pairs={{0,8},{8,0},{16,24},{24,16},{1,9},{9,1},{17,25},{25,17},{2,10},{10... | collective-permute-start | bytes 12296 | tf_op jit(solution)/shard_map/ppermute | solution.py:102
  15.6 26.3 %collective-permute-start.1 = (bf16[784,384]{1,0:T(8,128)(2,1)}, bf16[784,384]{1,0:T(8,128)(2,1)}, u32[]{:S(2)}, u32[]{:S(2)}) collective-permute-start(bf16[784,384]{1,0:T(8,128)(2,1)} %pad_maximum_fusion.27), channel_id=1, source_target_pairs={{0,4},{2,6},{4,0},{6,2},{1,5},{3,7},{5,1},{7,3},{8,12},{10,14},{12... | collective-permute-start | bytes 1806344 | tf_op jit(solution)/shard_map/ppermute | solution.py:102
  31.3 108.8 %collective-permute-start.28 = (bf16[256,768]{1,0:T(8,128)(2,1)}, bf16[256,768]{1,0:T(8,128)(2,1)}, u32[]{:S(2)}, u32[]{:S(2)}) collective-permute-start(bf16[256,768]{1,0:T(8,128)(2,1)} %slice.829), channel_id=1, source_target_pairs={{0,24},{8,16},{16,8},{24,0},{1,25},{9,17},{17,9},{25,1},{2,26},{10... | collective-permute-start | bytes 1179656 | tf_op jit(solution)/shard_map/ppermute | solution.py:102
  35.1 105.5 %collective-permute-start.26 = (bf16[256,768]{1,0:T(8,128)(2,1)}, bf16[256,768]{1,0:T(8,128)(2,1)}, u32[]{:S(2)}, u32[]{:S(2)}) collective-permute-start(bf16[256,768]{1,0:T(8,128)(2,1)} %slice.829), channel_id=1, source_target_pairs={{0,16},{8,24},{16,0},{24,8},{1,17},{9,25},{17,1},{25,9},{2,18},{10... | collective-permute-start | bytes 1179656 | tf_op jit(solution)/shard_map/ppermute | solution.py:102
  57.7 35.5 %collective-permute-start.4 = (bf16[2,512,384]{1,2,0:T(8,128)(2,1)S(1)}, bf16[2,512,384]{1,2,0:T(8,128)(2,1)S(1)}, u32[]{:S(2)}, u32[]{:S(2)}) collective-permute-start(bf16[2,512,384]{1,2,0:T(8,128)(2,1)S(1)} %slice.776), channel_id=1, source_target_pairs={{0,4},{2,6},{4,0},{6,2},{1,5},{3,7},{5,1},{7,3},{8,12},{10,14},{12... | collective-permute-start | bytes 2359304 | tf_op jit(solution)/shard_map/ppermute | solution.py:102
  58.9 34.4 %collective-permute-start.3 = (bf16[2,512,384]{1,2,0:T(8,128)(2,1)S(1)}, bf16[2,512,384]{1,2,0:T(8,128)(2,1)S(1)}, u32[]{:S(2)}, u32[]{:S(2)}) collective-permute-start(bf16[2,512,384]{1,2,0:T(8,128)(2,1)S(1)} %slice.776), channel_id=1, source_target_pairs={{0,2},{2,0},{4,6},{6,4},{1,3},{3,1},{5,7},{7,5},{8,10},{10,8},{12,... | collective-permute-start | bytes 2359304 | tf_op jit(solution)/shard_map/ppermute | solution.py:102
  77.3 63.5 %collective-permute-start.24 = (bf16[256,768]{1,0:T(8,128)(2,1)}, bf16[256,768]{1,0:T(8,128)(2,1)}, u32[]{:S(2)}, u32[]{:S(2)}) collective-permute-start(bf16[256,768]{1,0:T(8,128)(2,1)} %slice.829), channel_id=1, source_target_pairs={{0,8},{8,0},{16,24},{24,16},{1,9},{9,1},{17,25},{25,17},{2,10},{10... | collective-permute-start | bytes 1179656 | tf_op jit(solution)/shard_map/ppermute | solution.py:102
  152.5 33.8 %collective-permute-start.12 = (bf16[256,768]{1,0:T(8,128)(2,1)S(1)}, bf16[256,768]{1,0:T(8,128)(2,1)S(1)}, u32[]{:S(2)}, u32[]{:S(2)}) collective-permute-start(bf16[256,768]{1,0:T(8,128)(2,1)S(1)} %slice.802), channel_id=1, source_target_pairs={{0,16},{8,24},{16,0},{24,8},{1,17},{9,25},{17,1},{25,9},{2,18},{10... | collective-permute-start | bytes 1179656 | tf_op jit(solution)/shard_map/ppermute | solution.py:102
  152.5 33.8 %collective-permute-start.10 = (bf16[256,768]{1,0:T(8,128)(2,1)S(1)}, bf16[256,768]{1,0:T(8,128)(2,1)S(1)}, u32[]{:S(2)}, u32[]{:S(2)}) collective-permute-start(bf16[256,768]{1,0:T(8,128)(2,1)S(1)} %slice.802), channel_id=1, source_target_pairs={{0,8},{8,0},{16,24},{24,16},{1,9},{9,1},{17,25},{25,17},{2,10},{10... | collective-permute-start | bytes 1179656 | tf_op jit(solution)/shard_map/ppermute | solution.py:102
  154.9 55.2 %collective-permute-start.18 = (bf16[4,192,1536]{2,1,0:T(8,128)(2,1)S(1)}, bf16[4,192,1536]{2,1,0:T(8,128)(2,1)S(1)}, u32[]{:S(2)}, u32[]{:S(2)}) collective-permute-start(bf16[4,192,1536]{2,1,0:T(8,128)(2,1)S(1)} %pad_maximum_fusion.4), channel_id=1, source_target_pairs={{0,6},{2,4},{4,2},{6,0},{1,7},{3,5},{5,3},{7,1},{8,14},{10,12},{12... | collective-permute-start | bytes 7077896 | tf_op jit(solution)/shard_map/ppermute | solution.py:102
  187.0 71.9 %collective-permute-start.17 = (bf16[4,192,1536]{2,1,0:T(8,128)(2,1)S(1)}, bf16[4,192,1536]{2,1,0:T(8,128)(2,1)S(1)}, u32[]{:S(2)}, u32[]{:S(2)}) collective-permute-start(bf16[4,192,1536]{2,1,0:T(8,128)(2,1)S(1)} %pad_maximum_fusion.4), channel_id=1, source_target_pairs={{0,4},{2,6},{4,0},{6,2},{1,5},{3,7},{5,1},{7,3},{8,12},{10,14},{12... | collective-permute-start | bytes 7077896 | tf_op jit(solution)/shard_map/ppermute | solution.py:102
  188.5 70.6 %collective-permute-start.16 = (bf16[4,192,1536]{2,1,0:T(8,128)(2,1)S(1)}, bf16[4,192,1536]{2,1,0:T(8,128)(2,1)S(1)}, u32[]{:S(2)}, u32[]{:S(2)}) collective-permute-start(bf16[4,192,1536]{2,1,0:T(8,128)(2,1)S(1)} %pad_maximum_fusion.4), channel_id=1, source_target_pairs={{0,2},{2,0},{4,6},{6,4},{1,3},{3,1},{5,7},{7,5},{8,10},{10,8},{12,... | collective-permute-start | bytes 7077896 | tf_op jit(solution)/shard_map/ppermute | solution.py:102
  325.8 28.3 %collective-permute-start.62 = (bf16[192,1536]{1,0:T(8,128)(2,1)S(1)}, bf16[192,1536]{1,0:T(8,128)(2,1)S(1)}, u32[]{:S(2)}, u32[]{:S(2)}) collective-permute-start(bf16[192,1536]{1,0:T(8,128)(2,1)S(1)} %get-tuple-element.94), channel_id=1, source_target_pairs={{0,6},{2,4},{4,2},{6,0},{1,7},{3,5},{5,3},{7,1},{8,14},{10,12},{12... | collective-permute-start | bytes 1769480 | tf_op jit(solution)/shard_map/ppermute | solution.py:102
  334.2 29.0 %collective-permute-start.61 = (bf16[192,1536]{1,0:T(8,128)(2,1)S(1)}, bf16[192,1536]{1,0:T(8,128)(2,1)S(1)}, u32[]{:S(2)}, u32[]{:S(2)}) collective-permute-start(bf16[192,1536]{1,0:T(8,128)(2,1)S(1)} %get-tuple-element.95), channel_id=1, source_target_pairs={{0,4},{2,6},{4,0},{6,2},{1,5},{3,7},{5,1},{7,3},{8,12},{10,14},{12... | collective-permute-start | bytes 1769480 | tf_op jit(solution)/shard_map/ppermute | solution.py:102
  334.9 31.0 %collective-permute-start.66 = (bf16[192,1536]{1,0:T(8,128)(2,1)S(1)}, bf16[192,1536]{1,0:T(8,128)(2,1)S(1)}, u32[]{:S(2)}, u32[]{:S(2)}) collective-permute-start(bf16[192,1536]{1,0:T(8,128)(2,1)S(1)} %get-tuple-element.87), channel_id=1, source_target_pairs={{0,2},{2,0},{4,6},{6,4},{1,3},{3,1},{5,7},{7,5},{8,10},{10,8},{12,... | collective-permute-start | bytes 1769480 | tf_op jit(solution)/shard_map/ppermute | solution.py:102
  338.2 41.2 %collective-permute-start.68 = (bf16[192,1536]{1,0:T(8,128)(2,1)S(1)}, bf16[192,1536]{1,0:T(8,128)(2,1)S(1)}, u32[]{:S(2)}, u32[]{:S(2)}) collective-permute-start(bf16[192,1536]{1,0:T(8,128)(2,1)S(1)} %get-tuple-element.88), channel_id=1, source_target_pairs={{0,6},{2,4},{4,2},{6,0},{1,7},{3,5},{5,3},{7,1},{8,14},{10,12},{12... | collective-permute-start | bytes 1769480 | tf_op jit(solution)/shard_map/ppermute | solution.py:102
  340.5 47.9 %collective-permute-start.67 = (bf16[192,1536]{1,0:T(8,128)(2,1)S(1)}, bf16[192,1536]{1,0:T(8,128)(2,1)S(1)}, u32[]{:S(2)}, u32[]{:S(2)}) collective-permute-start(bf16[192,1536]{1,0:T(8,128)(2,1)S(1)} %get-tuple-element.89), channel_id=1, source_target_pairs={{0,4},{2,6},{4,0},{6,2},{1,5},{3,7},{5,1},{7,3},{8,12},{10,14},{12... | collective-permute-start | bytes 1769480 | tf_op jit(solution)/shard_map/ppermute | solution.py:102
  354.1 58.1 %collective-permute-start.30 = (bf16[4,256,768]{2,1,0:T(8,128)(2,1)S(1)}, bf16[4,256,768]{2,1,0:T(8,128)(2,1)S(1)}, u32[]{:S(2)}, u32[]{:S(2)}) collective-permute-start(bf16[4,256,768]{2,1,0:T(8,128)(2,1)S(1)} %fusion.53), channel_id=1, source_target_pairs={{0,1},{1,0},{2,3},{3,2},{4,5},{5,4},{6,7},{7,6},{8,9},{9,8},{10,11... | collective-permute-start | bytes 4718600 | tf_op jit(solution)/shard_map/ppermute | solution.py:102
  363.2 28.0 %collective-permute-start.57 = (bf16[192,1536]{1,0:T(8,128)(2,1)S(1)}, bf16[192,1536]{1,0:T(8,128)(2,1)S(1)}, u32[]{:S(2)}, u32[]{:S(2)}) collective-permute-start(bf16[192,1536]{1,0:T(8,128)(2,1)S(1)} %get-tuple-element.90), channel_id=1, source_target_pairs={{0,2},{2,0},{4,6},{6,4},{1,3},{3,1},{5,7},{7,5},{8,10},{10,8},{12,... | collective-permute-start | bytes 1769480 | tf_op jit(solution)/shard_map/ppermute | solution.py:102
  365.9 38.9 %collective-permute-start.59 = (bf16[192,1536]{1,0:T(8,128)(2,1)S(1)}, bf16[192,1536]{1,0:T(8,128)(2,1)S(1)}, u32[]{:S(2)}, u32[]{:S(2)}) collective-permute-start(bf16[192,1536]{1,0:T(8,128)(2,1)S(1)} %get-tuple-element.91), channel_id=1, source_target_pairs={{0,6},{2,4},{4,2},{6,0},{1,7},{3,5},{5,3},{7,1},{8,14},{10,12},{12... | collective-permute-start | bytes 1769480 | tf_op jit(solution)/shard_map/ppermute | solution.py:102
  379.4 31.9 %collective-permute-start.58 = (bf16[192,1536]{1,0:T(8,128)(2,1)S(1)}, bf16[192,1536]{1,0:T(8,128)(2,1)S(1)}, u32[]{:S(2)}, u32[]{:S(2)}) collective-permute-start(bf16[192,1536]{1,0:T(8,128)(2,1)S(1)} %get-tuple-element.92), channel_id=1, source_target_pairs={{0,4},{2,6},{4,0},{6,2},{1,5},{3,7},{5,1},{7,3},{8,12},{10,14},{12... | collective-permute-start | bytes 1769480 | tf_op jit(solution)/shard_map/ppermute | solution.py:102
  391.2 26.0 %collective-permute-start.63 = (bf16[192,1536]{1,0:T(8,128)(2,1)S(1)}, bf16[192,1536]{1,0:T(8,128)(2,1)S(1)}, u32[]{:S(2)}, u32[]{:S(2)}) collective-permute-start(bf16[192,1536]{1,0:T(8,128)(2,1)S(1)} %get-tuple-element.84), channel_id=1, source_target_pairs={{0,2},{2,0},{4,6},{6,4},{1,3},{3,1},{5,7},{7,5},{8,10},{10,8},{12,... | collective-permute-start | bytes 1769480 | tf_op jit(solution)/shard_map/ppermute | solution.py:102
  413.5 26.8 %collective-permute-start.31 = (bf16[256,768]{1,0:T(8,128)(2,1)S(1)}, bf16[256,768]{1,0:T(8,128)(2,1)S(1)}, u32[]{:S(2)}, u32[]{:S(2)}) collective-permute-start(bf16[256,768]{1,0:T(8,128)(2,1)S(1)} %get-tuple-element.122), channel_id=1, source_target_pairs={{0,8},{8,0},{16,24},{24,16},{1,9},{9,1},{17,25},{25,17},{2,10},{10... | collective-permute-start | bytes 1179656 | tf_op jit(solution)/shard_map/ppermute | solution.py:102
  415.6 74.0 %collective-permute-start.20 = (bf16[256,768]{1,0:T(8,128)(2,1)S(1)}, bf16[256,768]{1,0:T(8,128)(2,1)S(1)}, u32[]{:S(2)}, u32[]{:S(2)}) collective-permute-start(bf16[256,768]{1,0:T(8,128)(2,1)S(1)} %get-tuple-element.125), channel_id=1, source_target_pairs={{0,8},{8,0},{16,24},{24,16},{1,9},{9,1},{17,25},{25,17},{2,10},{10... | collective-permute-start | bytes 1179656 | tf_op jit(solution)/shard_map/ppermute | solution.py:102
  417.2 72.4 %collective-permute-start.22 = (bf16[256,768]{1,0:T(8,128)(2,1)S(1)}, bf16[256,768]{1,0:T(8,128)(2,1)S(1)}, u32[]{:S(2)}, u32[]{:S(2)}) collective-permute-start(bf16[256,768]{1,0:T(8,128)(2,1)S(1)} %get-tuple-element.126), channel_id=1, source_target_pairs={{0,24},{8,16},{16,8},{24,0},{1,25},{9,17},{17,9},{25,1},{2,26},{10... | collective-permute-start | bytes 1179656 | tf_op jit(solution)/shard_map/ppermute | solution.py:102
  429.2 60.5 %collective-permute-start.21 = (bf16[256,768]{1,0:T(8,128)(2,1)S(1)}, bf16[256,768]{1,0:T(8,128)(2,1)S(1)}, u32[]{:S(2)}, u32[]{:S(2)}) collective-permute-start(bf16[256,768]{1,0:T(8,128)(2,1)S(1)} %get-tuple-element.127), channel_id=1, source_target_pairs={{0,16},{8,24},{16,0},{24,8},{1,17},{9,25},{17,1},{25,9},{2,18},{10... | collective-permute-start | bytes 1179656 | tf_op jit(solution)/shard_map/ppermute | solution.py:102
  440.4 49.0 %collective-permute-start.32 = (bf16[256,768]{1,0:T(8,128)(2,1)S(1)}, bf16[256,768]{1,0:T(8,128)(2,1)S(1)}, u32[]{:S(2)}, u32[]{:S(2)}) collective-permute-start(bf16[256,768]{1,0:T(8,128)(2,1)S(1)} %get-tuple-element.124), channel_id=1, source_target_pairs={{0,16},{8,24},{16,0},{24,8},{1,17},{9,25},{17,1},{25,9},{2,18},{10... | collective-permute-start | bytes 1179656 | tf_op jit(solution)/shard_map/ppermute | solution.py:102
  558.9 36.2 %collective-permute-start.41 = (bf16[2,512,384]{2,1,0:T(8,128)(2,1)}, bf16[2,512,384]{2,1,0:T(8,128)(2,1)}, u32[]{:S(2)}, u32[]{:S(2)}) collective-permute-start(bf16[2,512,384]{2,1,0:T(8,128)(2,1)} %get-tuple-element.80), channel_id=1, source_target_pairs={{0,6},{2,4},{4,2},{6,0},{1,7},{3,5},{5,3},{7,1},{8,14},{10,12},{12... | collective-permute-start | bytes 2359304 | tf_op jit(solution)/shard_map/ppermute | solution.py:102
  560.4 36.1 %collective-permute-start.40 = (bf16[2,512,384]{2,1,0:T(8,128)(2,1)}, bf16[2,512,384]{2,1,0:T(8,128)(2,1)}, u32[]{:S(2)}, u32[]{:S(2)}) collective-permute-start(bf16[2,512,384]{2,1,0:T(8,128)(2,1)} %get-tuple-element.81), channel_id=1, source_target_pairs={{0,4},{2,6},{4,0},{6,2},{1,5},{3,7},{5,1},{7,3},{8,12},{10,14},{12... | collective-permute-start | bytes 2359304 | tf_op jit(solution)/shard_map/ppermute | solution.py:102
  610.2 25.7 %collective-permute-start.49 = (bf16[768,384]{1,0:T(8,128)(2,1)}, bf16[768,384]{1,0:T(8,128)(2,1)}, u32[]{:S(2)}, u32[]{:S(2)}) collective-permute-start(bf16[768,384]{1,0:T(8,128)(2,1)} %maximum_maximum_fusion.2), channel_id=1, source_target_pairs={{0,4},{2,6},{4,0},{6,2},{1,5},{3,7},{5,1},{7,3},{8,12},{10,14},{12... | collective-permute-start | bytes 1769480 | tf_op jit(solution)/shard_map/ppermute | solution.py:102
  620.9 46.1 %collective-permute-start.42 = (f32[512,768]{1,0:T(8,128)}, f32[512,768]{1,0:T(8,128)}, u32[]{:S(2)}, u32[]{:S(2)}) collective-permute-start(f32[512,768]{1,0:T(8,128)} %convolution_bitcast_fusion), channel_id=1, source_target_pairs={{0,1},{1,0},{2,3},{3,2},{4,5},{5,4},{6,7},{7,6},{8,9},{9,8},{10,11... | collective-permute-start | bytes 4718600 | tf_op jit(solution)/shard_map/ppermute | solution.py:102
  (145 other events, 1633.6 us)

commit v2 on v1

--- a/solution.py
+++ b/solution.py
@@ -3,10 +3,13 @@
 import jax
 import jax.numpy as jnp
 from jax import lax
+from jax.experimental import pallas as pl
+from jax.experimental.pallas import tpu as pltpu
 from jax.sharding import PartitionSpec as P
 
 D = 768
 HD = 64
+CHUNK = 128
 
 
 epsilon = 1e-06
@@ -19,79 +22,185 @@
     )
 
 
-def pair_of(array, num):
-    return array[:, 2 * HD * num : 2 * HD * (num + 1)].reshape(array.shape[0], 2, HD)
-
-
-def pair_scores(query_blk, keys_pair, slope_pair, decay_term):
-    raw_scores = jnp.einsum("qhd,khd->hqk", query_blk, keys_pair, preferred_element_type=jnp.float32)
-    return raw_scores * (1.0 / math.sqrt(HD)) - slope_pair[:, None, None] * decay_term[None]
-
-
-def pair_probs(scores):
-    exp_scores = jnp.exp(scores - jnp.max(scores, axis=-1, keepdims=True))
-    return exp_scores / jnp.sum(exp_scores, axis=-1, keepdims=True)
+def attend_kernel(slopes_ref, q_ref, k_ref, v_ref, decay_ref, out_ref, log_sum_ref):
+    pair = pl.program_id(0)
+    keys = k_ref[...]
+    values = v_ref[...]
+    lane = lax.broadcasted_iota(jnp.int32, (CHUNK, 2 * HD), 1)
+
+    def one_chunk(num, carry):
+        rows = pl.ds(pl.multiple_of(num * CHUNK, CHUNK), CHUNK)
+        query = q_ref[rows, :].astype(jnp.float32) * (1.0 / math.sqrt(HD))
+        decay = decay_ref[rows, :]
+        outs = []
+        log_sums = []
+        for head in range(2):
+            own = lane // HD == head
+            scores = lax.dot_general(
+                jnp.where(own, query, 0.0).astype(jnp.bfloat16),
+                keys,
+                (((1,), (1,)), ((), ())),
+                preferred_element_type=jnp.float32,
+            )
+            scores = scores - slopes_ref[2 * pair + head] * decay
+            top = jnp.max(scores, axis=1, keepdims=True)
+            exps = jnp.exp(scores - top)
+            total = jnp.sum(exps, axis=1, keepdims=True)
+            out = jnp.dot(exps.astype(jnp.bfloat16), values, preferred_element_type=jnp.float32)
+            outs.append(out / total)
+            log_sums.append(top + jnp.log(total))
+        out_ref[rows, :] = jnp.where(lane < HD, outs[0], outs[1]).astype(jnp.bfloat16)
+        log_sum_ref[rows, :] = jnp.where(lane < HD, log_sums[0], log_sums[1])
+        return carry
+
+    lax.fori_loop(0, q_ref.shape[0] // CHUNK, one_chunk, 0)
+
+
+def attend_back_kernel(
+    slopes_ref,
+    q_ref,
+    k_ref,
+    v_ref,
+    decay_ref,
+    log_sum_ref,
+    grad_ref,
+    dq_ref,
+    dk_ref,
+    dv_ref,
+    slope_ref,
+    dk_sum,
+    dv_sum,
+):
+    pair = pl.program_id(0)
+    scale = 1.0 / math.sqrt(HD)
+    keys = k_ref[...]
+    values = v_ref[...]
+    lane = lax.broadcasted_iota(jnp.int32, (CHUNK, 2 * HD), 1)
+    dk_sum[...] = jnp.zeros_like(dk_sum)
+    dv_sum[...] = jnp.zeros_like(dv_sum)
+    rows_last = (((1,), (1,)), ((), ()))
+    rows_first = (((0,), (0,)), ((), ()))
+
+    def one_chunk(num, slope_sums):
+        rows = pl.ds(pl.multiple_of(num * CHUNK, CHUNK), CHUNK)
+        query = q_ref[rows, :].astype(jnp.float32) * scale
+        grad = grad_ref[rows, :].astype(jnp.float32)
+        log_sum = log_sum_ref[rows, :]
+        decay = decay_ref[rows, :]
+        dqs = []
+        new_sums = []
+        for head in range(2):
+            own = lane // HD == head
+            query_own = jnp.where(own, query, 0.0).astype(jnp.bfloat16)
+            grad_own = jnp.where(own, grad, 0.0).astype(jnp.bfloat16)
+            scores = lax.dot_general(
+                query_own, keys, rows_last, preferred_element_type=jnp.float32
+            )
+            scores = scores - slopes_ref[2 * pair + head] * decay
+            probs = jnp.exp(scores - log_sum[:, HD * head : HD * head + 1])
+            grad_probs = lax.dot_general(
+                grad_own, values, rows_last, preferred_element_type=jnp.float32
+            )
+            row_sum = jnp.sum(probs * grad_probs, axis=1, keepdims=True)
+            grad_scores = (probs * (grad_probs - row_sum)).astype(jnp.bfloat16)
+            dv_sum[...] += lax.dot_general(
+                probs.astype(jnp.bfloat16),
+                grad_own,
+                rows_first,
+                preferred_element_type=jnp.float32,
+            )
+            dk_sum[...] += lax.dot_general(
+                grad_scores, query_own, rows_first, preferred_element_type=jnp.float32
+            )
+            dqs.append(jnp.dot(grad_scores, keys, preferred_element_type=jnp.float32))
+            slope_part = jnp.sum(grad_scores.astype(jnp.float32) * decay, axis=0, keepdims=True)
+            new_sums.append(slope_sums[head] + slope_part)
+        dq_ref[rows, :] = (jnp.where(lane < HD, dqs[0], dqs[1]) * scale).astype(jnp.bfloat16)
+        return tuple(new_sums)
+
+    start = jnp.zeros((1, keys.shape[0]), jnp.float32)
+    sums = lax.fori_loop(0, q_ref.shape[0] // CHUNK, one_chunk, (start, start))
+    dk_ref[...] = dk_sum[...].astype(jnp.bfloat16)
+    dv_ref[...] = dv_sum[...].astype(jnp.bfloat16)
+    totals = [-jnp.sum(part, axis=1, keepdims=True) for part in sums]
+    row = lax.broadcasted_iota(jnp.int32, (8, 128), 0)
+    slope_ref[0] = jnp.where(row == 0, totals[0], totals[1])
+
+
+def attend_specs(rows, keys):
+    return {
+        "slopes": pl.BlockSpec(memory_space=pltpu.SMEM),
+        "rows": pl.BlockSpec((rows, 2 * HD), lambda p: (0, p)),
+        "keys": pl.BlockSpec((keys, 2 * HD), lambda p: (0, p)),
+        "decay": pl.BlockSpec((rows, keys), lambda p: (0, 0)),
+    }
+
+
+def attend_cost(rows, keys, heads, dots):
+    return pl.CostEstimate(
+        flops=2 * dots * heads * rows * keys * 2 * HD,
+        bytes_accessed=4 * rows * keys + 8 * heads * HD * keys,
+        transcendentals=heads * rows * keys,
+    )
 
 
 def attend(queries, keys_all, values_all, slopes, decay_term):
-    out_cols = []
-    for num in range(queries.shape[1] // (2 * HD)):
-        scores = pair_scores(
-            pair_of(queries, num), pair_of(keys_all, num), slopes[2 * num : 2 * num + 2], decay_term
-        )
-        out_cols.append(
-            jnp.einsum(
-                "hqk,khd->qhd",
-                pair_probs(scores).astype(jnp.bfloat16),
-                pair_of(values_all, num),
-                preferred_element_type=jnp.float32,
-            ).reshape(queries.shape[0], 2 * HD)
-        )
-    return jnp.concatenate(out_cols, axis=1).astype(jnp.bfloat16)
-
-
-def attend_back(queries, keys_all, values_all, slopes, decay_term, grad_att):
-    scale = 1.0 / math.sqrt(HD)
-    grad_cols = ([], [], [])
-    slope_cols = []
-
-    def flat(values):
-        return values.reshape(values.shape[0], 2 * HD).astype(jnp.bfloat16)
-
-    for num in range(queries.shape[1] // (2 * HD)):
-        query_blk, keys_pair, values_pair, grad_blk = [
-            pair_of(array, num) for array in (queries, keys_all, values_all, grad_att)
-        ]
-        probs = pair_probs(
-            pair_scores(query_blk, keys_pair, slopes[2 * num : 2 * num + 2], decay_term)
-        )
-        grad_probs = jnp.einsum(
-            "qhd,khd->hqk", grad_blk, values_pair, preferred_element_type=jnp.float32
-        )
-        row_sum = jnp.sum(probs * grad_probs, axis=-1, keepdims=True)
-        grad_scores = (probs * (grad_probs - row_sum)).astype(jnp.bfloat16)
-        query_part = jnp.einsum(
-            "hqk,khd->qhd", grad_scores, keys_pair, preferred_element_type=jnp.float32
-        )
-        key_part = jnp.einsum(
-            "hqk,qhd->khd", grad_scores, query_blk, preferred_element_type=jnp.float32
-        )
-        value_part = jnp.einsum(
-            "hqk,qhd->khd",
-            probs.astype(jnp.bfloat16),
-            grad_blk,
-            preferred_element_type=jnp.float32,
-        )
-        grad_cols[0].append(flat(query_part * scale))
-        grad_cols[1].append(flat(key_part * scale))
-        grad_cols[2].append(flat(value_part))
-        slope_cols.append(
-            -jnp.sum(grad_scores.astype(jnp.float32) * decay_term[None], axis=(1, 2))
-        )
-    return (
-        *[jnp.concatenate(cols, axis=1) for cols in grad_cols],
-        jnp.concatenate(slope_cols),
-    )
+    rows, columns = queries.shape
+    keys = keys_all.shape[0]
+    spec = attend_specs(rows, keys)
+    return pl.pallas_call(
+        attend_kernel,
+        grid=(columns // (2 * HD),),
+        in_specs=[spec["slopes"], spec["rows"], spec["keys"], spec["keys"], spec["decay"]],
+        out_specs=[spec["rows"], spec["rows"]],
+        out_shape=[
+            jax.ShapeDtypeStruct((rows, columns), jnp.bfloat16),
+            jax.ShapeDtypeStruct((rows, columns), jnp.float32),
+        ],
+        cost_estimate=attend_cost(rows, keys, columns // HD, 2),
+        compiler_params=pltpu.CompilerParams(vmem_limit_bytes=40 << 20),
+        name="attend",
+    )(slopes, queries, keys_all, values_all, decay_term)
+
+
+def attend_back(queries, keys_all, values_all, slopes, decay_term, log_sums, grad_att):
+    rows, columns = queries.shape
+    keys = keys_all.shape[0]
+    pairs = columns // (2 * HD)
+    spec = attend_specs(rows, keys)
+    dq, dk, dv, slope_tiles = pl.pallas_call(
+        attend_back_kernel,
+        grid=(pairs,),
+        in_specs=[
+            spec["slopes"],
+            spec["rows"],
+            spec["keys"],
+            spec["keys"],
+            spec["decay"],
+            spec["rows"],
+            spec["rows"],
+        ],
+        out_specs=[
+            spec["rows"],
+            spec["keys"],
+            spec["keys"],
+            pl.BlockSpec((1, 8, 128), lambda p: (p, 0, 0)),
+        ],
+        out_shape=[
+            jax.ShapeDtypeStruct((rows, columns), jnp.bfloat16),
+            jax.ShapeDtypeStruct((keys, columns), jnp.bfloat16),
+            jax.ShapeDtypeStruct((keys, columns), jnp.bfloat16),
+            jax.ShapeDtypeStruct((pairs, 8, 128), jnp.float32),
+        ],
+        scratch_shapes=[
+            pltpu.VMEM((keys, 2 * HD), jnp.float32),
+            pltpu.VMEM((keys, 2 * HD), jnp.float32),
+        ],
+        cost_estimate=attend_cost(rows, keys, columns // HD, 5),
+        compiler_params=pltpu.CompilerParams(vmem_limit_bytes=48 << 20),
+        name="attend_back",
+    )(slopes, queries, keys_all, values_all, decay_term, log_sums, grad_att)
+    return dq, dk, dv, slope_tiles[:, :2, 0].reshape(-1)
 
 
 def swap_pairs(axis, step):
@@ -111,6 +220,44 @@
     for s in range(1, lax.axis_size(axis)):
         total = total + hop(chunks[s], axis, s).astype(jnp.float32)
     return total
+
+
+def square_pieces(values, axis):
+    if lax.axis_size(axis) != 4:
+        return pieces_of(values, axis)
+    cut = values.shape[0] // 2
+    first, second = values[:cut], values[cut:]
+    first_by = [first, hop(first, axis, 1), None, None]
+    second_by = [second, None, hop(second, axis, 2), None]
+    for s in (0, 1):
+        first_by[s + 2] = hop(first_by[s], axis, 2)
+    for s in (0, 2):
+        second_by[s + 1] = hop(second_by[s], axis, 1)
+    return [jnp.concatenate(both, axis=0) for both in zip(first_by, second_by)]
+
+
+def square_hops(chunks, axis):
+    cut = chunks[0].shape[0] // 2
+    first = [chunk[:cut] for chunk in chunks]
+    second = [chunk[cut:] for chunk in chunks]
+    near = (first[1] + hop(first[3], axis, 2)).astype(jnp.bfloat16)
+    side = (second[2] + hop(second[3], axis, 1)).astype(jnp.bfloat16)
+    return [
+        first[0],
+        hop(first[2], axis, 2),
+        hop(near, axis, 1),
+        second[0],
+        hop(second[1], axis, 1),
+        hop(side, axis, 2),
+    ]
+
+
+def summed_square(found):
+    halves = []
+    for parts in (found[:3], found[3:]):
+        parts = [part.astype(jnp.float32) for part in parts]
+        halves.append(parts[0] + parts[1] + parts[2])
+    return jnp.concatenate(halves, axis=0)
 
 
 def summed_everywhere(values, axis):
@@ -213,7 +360,7 @@
         ],
         axis=0,
     )
-    packs = pieces_of(pack, "width")
+    packs = square_pieces(pack, "width")
     out_from = 3 * block_d
     small_from = out_from + out_weight.shape[0] // 2
     w_qkv = jnp.concatenate(
@@ -236,7 +383,7 @@
         jnp.bfloat16
     )
     queries = qkv_vals[0]
-    kv_pieces = pieces_of(qkv_vals[1:], "width")
+    kv_pieces = square_pieces(qkv_vals[1:], "width")
     expert_stack = jnp.concatenate(
         [expert_in, jnp.swapaxes(expert_out, 1, 2).astype(jnp.bfloat16)], axis=0
     )
@@ -244,7 +391,7 @@
     key_value = jnp.concatenate(kv_pieces, axis=1)
     keys_all = key_value[0]
     values_all = key_value[1]
-    stacks = pieces_of(expert_stack, "width")
+    stacks = square_pieces(expert_stack, "width")
     w_first = [
         jnp.concatenate([piece[e] for piece in stacks], axis=0) for e in range(local_experts)
     ]
@@ -267,7 +414,7 @@
     allowed = (seg_query[:, None] == seg_all[None, :]) & (key_pos[None, :] <= query_pos[:, None])
     decay_term = jnp.where(allowed, jnp.log1p(distance.astype(jnp.float32)), 1e30)
 
-    attended = attend(queries, keys_all, values_all, slopes, decay_term)
+    attended, log_sums = attend(queries, keys_all, values_all, slopes, decay_term)
     proj_part = jnp.dot(attended, w_proj, preferred_element_type=jnp.float32)
     hidden_one = x_vals + (proj_part + hop(proj_part, "heads", 1))
     norm_second, back_second = jax.vjp(rms_norm, hidden_one, gain_two)
@@ -292,8 +439,7 @@
     slots_y = []
     slots_back = []
     gate_rows = []
-    sums_in = []
-    sums_out = []
+    sums_found = []
     for e in range(local_experts):
         expert_id = dp_index * local_experts + e
         named = [routes_all[:, k] == expert_id for k in range(2)]
@@ -337,13 +483,14 @@
             rows_in, grad_pre, (((0,), (0,)), ((), ())), preferred_element_type=jnp.float32
         ).astype(jnp.bfloat16)
         cut = [slice(s * block_d, (s + 1) * block_d) for s in range(width_count)]
-        sums_in.append(summed_pieces([grad_first[c] for c in cut], "width"))
-        sums_out.append(summed_pieces([grad_second[c] for c in cut], "width"))
-    expert_in_grad = jnp.stack(sums_in)
-    expert_out_grad = jnp.swapaxes(jnp.stack(sums_out), 1, 2)
-
+        sums_found.append(
+            square_hops(
+                [jnp.concatenate([grad_first[c], grad_second[c]], axis=0) for c in cut], "width"
+            )
+        )
     all_picks = jnp.concatenate(slots_picks, axis=1)
     grad_xn_own = rows_returned(all_picks, jnp.concatenate(slots_back, axis=1), half)
+    grad_xn_own, slots_y = lax.optimization_barrier((grad_xn_own, slots_y))
     mixed_own = rows_returned(all_picks, jnp.concatenate(slots_y, axis=1), half)
     hidden_own = lax.dynamic_slice_in_dim(hidden_one, head_index * half, half, 0)
     mixed_low = (hidden_own + mixed_own).astype(jnp.bfloat16)
@@ -384,12 +531,21 @@
         grad_branch, w_proj, (((1,), (1,)), ((), ())), preferred_element_type=jnp.float32
     ).astype(jnp.bfloat16)
     query_grad, key_grad, value_grad, slope_grad = attend_back(
-        queries, keys_all, values_all, slopes, decay_term, grad_att
-    )
-    kv_both = jnp.stack([key_grad, value_grad]).astype(jnp.bfloat16)
-    kv_grad = summed_pieces(
-        [kv_both[:, s * rows_own : (s + 1) * rows_own] for s in range(width_count)], "width"
+        queries, keys_all, values_all, slopes, decay_term, log_sums, grad_att
+    )
+    sums_found, key_grad, value_grad = lax.optimization_barrier((sums_found, key_grad, value_grad))
+    kv_grad = summed_square(
+        square_hops(
+            [
+                jnp.stack([part[s * rows_own : (s + 1) * rows_own] for part in (key_grad, value_grad)])
+                for s in range(width_count)
+            ],
+            "width",
+        )
     ).astype(jnp.bfloat16)
+    expert_sums = jnp.stack([summed_square(found) for found in sums_found])
+    expert_in_grad = expert_sums[:, :block_d]
+    expert_out_grad = jnp.swapaxes(expert_sums[:, block_d:], 1, 2)
     qkv_cot = jnp.concatenate([query_grad[None], kv_grad], axis=0)
     grad_xn_part = jnp.einsum("jrc,jdc->rd", qkv_cot, w_qkv, preferred_element_type=jnp.float32)
     grad_xn_one = grad_xn_part + hop(grad_xn_part, "heads", 1)
@@ -409,7 +565,11 @@
         )
         for c in cut
     ]
-    own_grads = summed_pieces(grad_chunks, "width").astype(jnp.bfloat16)
+    own_grads = summed_square(square_hops(grad_chunks, "width")).astype(jnp.bfloat16)
+    tiny = jnp.concatenate([router_full_t, gain_one_grad[None], gain_two_grad[None]], axis=0)
+    slope_row = jnp.pad(slope_grad, (0, block_d - slope_grad.shape[0]))[None]
+    tiny_sum = summed_pieces([jnp.concatenate([tiny[:, c], slope_row], axis=0) for c in cut], "width")
+    tiny_sum = summed_everywhere(tiny_sum, "dp")
     part_rows = own_grads.shape[0] // dp_count
 
     def part_of(s):
@@ -423,10 +583,6 @@
     qkv_grad = grads[:out_from].reshape(3, block_d, heads_cols)
     out_grad = unbeside(grads[out_from:])
 
-    tiny = jnp.concatenate([router_full_t, gain_one_grad[None], gain_two_grad[None]], axis=0)
-    slope_row = jnp.pad(slope_grad, (0, block_d - slope_grad.shape[0]))[None]
-    tiny_sum = summed_pieces([jnp.concatenate([tiny[:, c], slope_row], axis=0) for c in cut], "width")
-    tiny_sum = summed_everywhere(tiny_sum, "dp")
     return (
         mixed_out,
         input_grad,

time: 697 us -> 479 us (0.69)
  waiting for transfers between devices: 314 us -> 147 us
  matrix products: 159 us -> 90.5 us
  Pallas kernels: 0 us -> 49.9 us
  local copies, waits for them, and re-layouts: 58.9 us -> 38.7 us
  other arithmetic: 71 us -> 55.1 us
  starting transfers between devices: 80.7 us -> 89.4 us
    ppermute x69 -> x84, waiting for transfers between devices: 314 us -> 147 us  [hop(): return lax.ppermute(values, axis, swap_pairs(axis, step))]
    pallas_call x0 -> x2, Pallas kernels: none -> 49.9 us  [the longest x1 31.4 us: attend_back(): pl.pallas_call(attend_back_kernel, grid=(pairs,), in_specs=[spec['slopes'...]
    dot_general x15 -> x0, matrix products: 40.7 us -> none  [the longest x3 14.9 us: attend(): jnp.einsum('hqk,khd->qhd', pair_probs(scores).astype(jnp.bfloat16), pair_...]
    sub x3 -> x0, matrix products: 27.1 us -> none  [pair_probs(): exp_scores = jnp.exp(scores - jnp.max(scores, axis=-1, keepdims=True))]
    reduce_sum x1 -> x0, other arithmetic: 20.6 us -> none  [attend_back(): jnp.sum(grad_scores.astype(jnp.float32) * decay_term[None], axis=(1, 2))]
    convert_element_type x9 -> x0, local copies, waits for them, and re-layouts: 9.14 us -> none  [flat(): return values.reshape(values.shape[0], 2 * HD).astype(jnp.bfloat16)]
    ppermute x69 -> x84, starting transfers between devices: 80.7 us -> 89.4 us  [hop(): return lax.ppermute(values, axis, swap_pairs(axis, step))]
  transfers between devices with their start and end apart: 69 -> 84, of which waited for: 36 -> 31; matrix products, arithmetic and copies ran while one was open for 21% -> 23% of each run, Pallas kernels for 0% -> 11%
where the time goes in v2:
time: 479 us; the launch traced here: 473 us
  waiting for transfers between devices  147 us (31%)
  matrix products  90.5 us (19%)
  starting transfers between devices  89.4 us (19%)
  other arithmetic  55.1 us (12%)
  Pallas kernels  49.9 us (10%)
  local copies, waits for them, and re-layouts  38.7 us (8%)
    ppermute x84, waiting for transfers between devices, hop(): return lax.ppermute(values, axis, swap_pairs(axis, step))  147 us
    ppermute x84, starting transfers between devices, hop(): return lax.ppermute(values, axis, swap_pairs(axis, step))  89.4 us
    pallas_call x1, Pallas kernels, attend_back(): pl.pallas_call(attend_back_kernel, grid=(pairs,), in_specs=[spec['slopes'...  31.4 us
    pallas_call x1, Pallas kernels, attend(): pl.pallas_call(attend_kernel, grid=(columns // (2 * HD),), in_specs=[spec...  18.5 us
    dot_general x2, matrix products, shards(): jnp.dot(grad_rows, w_second_t[e], preferred_element_type=jnp.float32)  15.7 us
    dot_general x2, matrix products, shards(): lax.dot_general(act_low, w_second_t[e], (((1,), (1,)), ((), ())), preferr...  13.2 us
    dot_general x2, matrix products, shards(): lax.dot_general(grad_rows, act_low, (((0,), (0,)), ((), ())), preferred_e...  11.4 us
    dot_general x2, matrix products, shards(): pre_act = jnp.dot(rows_in, w_first[e], preferred_element_type=jnp.float32)  9.9 us
  transfers between devices with their start and end apart: 84, of which 31 were waited for; matrix products, arithmetic and copies ran while one was open for 23% of the time, Pallas kernels for 11%

profile of v2, /device:TPU:0, one launch (start us, length us, event | category | flops | bytes accessed | tf_op | source)
XLA Modules:
  0.0 473.0 jit_solution(18339228863835646366)
XLA Ops:
  2.1 5.0 %collective-permute-start.15 = (s32[2,512]{1,0:T(2,128)S(1)}, s32[2,512]{1,0:T(2,128)S(1)}, u32[]{:S(2)}, u32[]{:S(2)}) collective-permute-start(s32[2,512]{1,0:T(2,128)S(1)} %add_select_fusion), channel_id=1, source_target_pairs={{0,24},{8,16},{16,8},{24,0},{1,25},{9,17},{17,9},{25,1},{2,26},{10... | collective-permute-start | bytes 12296 | tf_op jit(solution)/shard_map/ppermute | solution.py:211
  20.2 4.4 log-plus-one_select_fusion.decay_ref
  32.2 3.8 collective-permute-start.26
  56.0 11.9 %collective-permute-done.24 = bf16[256,768]{1,0:T(8,128)(2,1)} collective-permute-done((bf16[256,768]{1,0:T(8,128)(2,1)}, bf16[256,768]{1,0:T(8,128)(2,1)}, u32[]{:S(2)}, u32[]{:S(2)}) %collective-permute-start.24) | collective-permute-done | bytes 393248 | tf_op jit(solution)/shard_map/ppermute | solution.py:211
  84.5 5.4 %collective-permute-done.6 = bf16[1,512,384]{2,1,0:T(8,128)(2,1)S(1)} collective-permute-done((bf16[1,512,384]{2,1,0:T(8,128)(2,1)S(1)}, bf16[1,512,384]{2,1,0:T(8,128)(2,1)S(1)}, u32[]{:S(2)}, u32[]{:S(2)}) %collective-permute-start.6) | collective-permute-done | bytes 393248 | tf_op jit(solution)/shard_map/ppermute | solution.py:211
  90.4 6.4 %collective-permute-done.9 = bf16[1,512,384]{2,1,0:T(8,128)(2,1)S(1)} collective-permute-done((bf16[1,512,384]{2,1,0:T(8,128)(2,1)S(1)}, bf16[1,512,384]{2,1,0:T(8,128)(2,1)S(1)}, u32[]{:S(2)}, u32[]{:S(2)}) %collective-permute-start.9) | collective-permute-done | bytes 393248 | tf_op jit(solution)/shard_map/ppermute | solution.py:211
  100.1 4.2 collective-permute-done.10
  114.6 18.5 %attend.1 = (bf16[512,384]{1,0:T(8,128)(2,1)S(1)}, f32[512,384]{1,0:T(8,128)S(1)}) custom-call(f32[6]{0:T(128)S(1)} %copy-done.5, bf16[512,384]{1,0:T(8,128)(2,1)S(1)} %get-tuple-element.179.q_ref, bf16[2048,384]{1,0:T(8,128)(2,1)S(1)} %get-tuple-element.122.k_ref, bf16[2048,384]{1,0:T(8,128)(2,1)S(1)} %get-tuple-element.121.v_ref, f32[512,2048]{1,0:T(8,128)S(1)} %copy-done), custom_call_target="tpu_custom_call" | custom-call | flops 3221225472 | bytes 10485760 | tf_op jit(solution)/shard_map/attend/pallas_call | solution.py:151
  145.4 20.5 %collective-permute-done.31 = bf16[2,192,1536]{2,1,0:T(8,128)(2,1)S(1)} collective-permute-done((bf16[2,192,1536]{2,1,0:T(8,128)(2,1)S(1)}, bf16[2,192,1536]{2,1,0:T(8,128)(2,1)S(1)}, u32[]{:S(2)}, u32[]{:S(2)}) %collective-permute-start.31) | collective-permute-done | bytes 1179680 | tf_op jit(solution)/shard_map/ppermute | solution.py:211
  167.6 9.6 %collective-permute-done.18 = bf16[256,768]{1,0:T(8,128)(2,1)S(1)} collective-permute-done((bf16[256,768]{1,0:T(8,128)(2,1)S(1)}, bf16[256,768]{1,0:T(8,128)(2,1)S(1)}, u32[]{:S(2)}, u32[]{:S(2)}) %collective-permute-start.18) | collective-permute-done | bytes 393248 | tf_op jit(solution)/shard_map/ppermute | solution.py:211
  177.2 4.9 %collective-permute-done.16 = bf16[256,768]{1,0:T(8,128)(2,1)S(1)} collective-permute-done((bf16[256,768]{1,0:T(8,128)(2,1)S(1)}, bf16[256,768]{1,0:T(8,128)(2,1)S(1)}, u32[]{:S(2)}, u32[]{:S(2)}) %collective-permute-start.16) | collective-permute-done | bytes 393248 | tf_op jit(solution)/shard_map/ppermute | solution.py:211
  184.9 3.3 fusion.26
  188.3 3.3 fusion.27
  191.7 5.1 %fusion.60 = f32[1024,1536]{1,0:T(8,128)} fusion(bf16[1024,768]{1,0:T(8,128)(2,1)S(1)} %bitcast.304, bf16[192,1536]{1,0:T(8,128)(2,1)S(1)} %get-tuple-element.175, bf16[192,1536]{1,0:T(8,128)(2,1)S(1)} %get-tuple-element.173, bf16[192,1536]{1,0:T(8,128)(2,1)S(1)} %get-tuple-element.171, bf16[192,1536]{1,0:T(8,128)(2,1)S(1)} %get-tuple-element.138), kind=kOutput, calls=%fused_computation.190 | convolution fusion | flops 2425356288 | bytes 10223616 | tf_op jit(solution)/shard_map/dot_general | solution.py:463
  196.9 6.6 %fusion.61 = f32[1024,768]{1,0:T(8,128)S(1)} fusion(bf16[192,1536]{1,0:T(8,128)(2,1)S(1)} %get-tuple-element.169, bf16[192,1536]{1,0:T(8,128)(2,1)S(1)} %get-tuple-element.167, bf16[192,1536]{1,0:T(8,128)(2,1)S(1)} %get-tuple-element.165, bf16[192,1536]{1,0:T(8,128)(2,1)S(1)} %get-tuple-element.135, f32[1024,1536]{1,0:T(8,128)} %fusion.60), kind=kOutput, calls=%fused_computation.191 | convolution fusion | flops 2439512064 | bytes 11796480 | tf_op jit(solution)/shard_map/dot_general | solution.py:466
  205.4 7.8 %fusion.6 = bf16[1024,1536]{1,0:T(8,128)(2,1)S(1)} fusion(f32[1024,1536]{1,0:T(8,128)} %fusion.60, bf16[1024,768]{1,0:T(8,128)(2,1)S(1)} %bitcast.274, bf16[192,1536]{1,0:T(8,128)(2,1)S(1)} %get-tuple-element.169, bf16[192,1536]{1,0:T(8,128)(2,1)S(1)} %get-tuple-element.167, bf16[192,1536]{1,0:T(8,128)(2,1)S(1)} %get-tuple-element.165, ...), kind=kOutput, calls=%fused_computation.10 | convolution fusion | flops 2456813568 | bytes 13369344 | tf_op jit(solution)/shard_map/dot_general | solution.py:473
  213.2 5.7 %convolution_convert_fusion.2 = bf16[768,1536]{1,0:T(8,128)(2,1)S(1)} fusion(bf16[1024,768]{1,0:T(8,128)(2,1)S(1)} %bitcast.275, f32[1024,1536]{1,0:T(8,128)} %fusion.60), kind=kOutput, calls=%fused_computation.27 | convolution fusion | flops 2431254528 | bytes 10223616 | tf_op jit(solution)/shard_map/dot_general | solution.py:479
  224.6 4.8 %fusion.57 = f32[1024,1536]{1,0:T(8,128)} fusion(bf16[1024,768]{1,0:T(8,128)(2,1)S(1)} %bitcast.302, bf16[192,1536]{1,0:T(8,128)(2,1)S(1)} %get-tuple-element.176, bf16[192,1536]{1,0:T(8,128)(2,1)S(1)} %get-tuple-element.174, bf16[192,1536]{1,0:T(8,128)(2,1)S(1)} %get-tuple-element.172, bf16[192,1536]{1,0:T(8,128)(2,1)S(1)} %get-tuple-element.136), kind=kOutput, calls=%fused_computation.187 | convolution fusion | flops 2425356288 | bytes 10223616 | tf_op jit(solution)/shard_map/dot_general | solution.py:463
  229.4 6.6 %fusion.58 = f32[1024,768]{1,0:T(8,128)S(1)} fusion(bf16[192,1536]{1,0:T(8,128)(2,1)S(1)} %get-tuple-element.170, bf16[192,1536]{1,0:T(8,128)(2,1)S(1)} %get-tuple-element.168, bf16[192,1536]{1,0:T(8,128)(2,1)S(1)} %get-tuple-element.166, bf16[192,1536]{1,0:T(8,128)(2,1)S(1)} %get-tuple-element.137, f32[1024,1536]{1,0:T(8,128)} %fusion.57), kind=kOutput, calls=%fused_computation.188 | convolution fusion | flops 2439512064 | bytes 11796480 | tf_op jit(solution)/shard_map/dot_general | solution.py:466
  237.8 7.8 %fusion.13 = bf16[1024,1536]{1,0:T(8,128)(2,1)S(1)} fusion(f32[1024,1536]{1,0:T(8,128)} %fusion.57, bf16[1024,768]{1,0:T(8,128)(2,1)S(1)} %bitcast.276, bf16[192,1536]{1,0:T(8,128)(2,1)S(1)} %get-tuple-element.170, bf16[192,1536]{1,0:T(8,128)(2,1)S(1)} %get-tuple-element.168, bf16[192,1536]{1,0:T(8,128)(2,1)S(1)} %get-tuple-element.166, ...), kind=kOutput, calls=%fused_computation.17 | convolution fusion | flops 2456813568 | bytes 13369344 | tf_op jit(solution)/shard_map/dot_general | solution.py:473
  245.6 5.7 %convolution_convert_fusion = bf16[768,1536]{1,0:T(8,128)(2,1)S(1)} fusion(bf16[1024,768]{1,0:T(8,128)(2,1)S(1)} %bitcast.277, f32[1024,1536]{1,0:T(8,128)} %fusion.57), kind=kOutput, calls=%fused_computation.25 | convolution fusion | flops 2431254528 | bytes 10223616 | tf_op jit(solution)/shard_map/dot_general | solution.py:479
  279.9 5.4 %collective-permute-done.58 = bf16[192,1536]{1,0:T(8,128)(2,1)S(1)} collective-permute-done((bf16[192,1536]{1,0:T(8,128)(2,1)S(1)}, bf16[192,1536]{1,0:T(8,128)(2,1)S(1)}, u32[]{:S(2)}, u32[]{:S(2)}) %collective-permute-start.58) | collective-permute-done | bytes 589856 | tf_op jit(solution)/shard_map/ppermute | solution.py:211
  285.9 3.3 collective-permute-done.35
  290.0 8.5 %collective-permute-done.37 = bf16[256,768]{1,0:T(8,128)(2,1)S(1)} collective-permute-done((bf16[256,768]{1,0:T(8,128)(2,1)S(1)}, bf16[256,768]{1,0:T(8,128)(2,1)S(1)}, u32[]{:S(2)}, u32[]{:S(2)}) %collective-permute-start.37) | collective-permute-done | bytes 393248 | tf_op jit(solution)/shard_map/ppermute | solution.py:211
  299.0 13.4 %collective-permute-done.36 = bf16[256,768]{1,0:T(8,128)(2,1)S(1)} collective-permute-done((bf16[256,768]{1,0:T(8,128)(2,1)S(1)}, bf16[256,768]{1,0:T(8,128)(2,1)S(1)}, u32[]{:S(2)}, u32[]{:S(2)}) %collective-permute-start.36) | collective-permute-done | bytes 393248 | tf_op jit(solution)/shard_map/ppermute | solution.py:211
  323.1 31.4 %attend_back.1 = (bf16[512,384]{1,0:T(8,128)(2,1)S(1)}, bf16[2048,384]{1,0:T(8,128)(2,1)S(1)}, bf16[2048,384]{1,0:T(8,128)(2,1)S(1)}, f32[3,8,128]{2,1,0:T(8,128)S(1)}) custom-call(f32[6]{0:T(128)S(1)} %copy-done.5, bf16[512,384]{1,0:T(8,128)(2,1)S(1)} %get-tuple-element.179.q_ref, bf16[2048,384]{1,0:T(8,128)(2,1)} %copy-done.2, ...), custom_call_target="tpu_custom_call" | custom-call | flops 8053063680 | bytes 10485760 | tf_op jit(solution)/shard_map/attend_back/pallas_call | solution.py:171
  365.0 5.0 %fusion.15 = (f32[2,1536,192]{1,2,0:T(8,128)}, f32[2,192,1536]{2,1,0:T(8,128)}) fusion(f32[1,384,1536]{2,1,0:T(8,128)} %maximum_bitcast_fusion.1, f32[1,384,1536]{2,1,0:T(8,128)} %maximum_bitcast_fusion), kind=kLoop, calls=%fused_computation.49 | loop fusion | flops 1179648 | bytes 9437184 | tf_op jit(solution)/shard_map/transpose | solution.py:548
  370.7 5.3 %collective-permute-done.61 = bf16[1,512,384]{2,1,0:T(8,128)(2,1)} collective-permute-done((bf16[1,512,384]{2,1,0:T(8,128)(2,1)}, bf16[1,512,384]{2,1,0:T(8,128)(2,1)}, u32[]{:S(2)}, u32[]{:S(2)}) %collective-permute-start.61) | collective-permute-done | bytes 393248 | tf_op jit(solution)/shard_map/ppermute | solution.py:211
  395.4 4.1 collective-permute-done.73
  405.1 14.8 %collective-permute-done.40 = bf16[256,768]{1,0:T(8,128)(2,1)S(1)} collective-permute-done((bf16[256,768]{1,0:T(8,128)(2,1)S(1)}, bf16[256,768]{1,0:T(8,128)(2,1)S(1)}, u32[]{:S(2)}, u32[]{:S(2)}) %collective-permute-start.40) | collective-permute-done | bytes 393248 | tf_op jit(solution)/shard_map/ppermute | solution.py:211
  430.2 6.2 %collective-permute-done.79 = bf16[192,384]{1,0:T(8,128)(2,1)S(1)} collective-permute-done((bf16[192,384]{1,0:T(8,128)(2,1)S(1)}, bf16[192,384]{1,0:T(8,128)(2,1)S(1)}, u32[]{:S(2)}, u32[]{:S(2)}) %collective-permute-start.79) | collective-permute-done | bytes 147488 | tf_op jit(solution)/shard_map/ppermute | solution.py:211
  436.8 3.4 collective-permute-start.82
  (503 shorter events, 218.0 us)
Async XLA Ops:
  2.1 29.2 %collective-permute-start.15 = (s32[2,512]{1,0:T(2,128)S(1)}, s32[2,512]{1,0:T(2,128)S(1)}, u32[]{:S(2)}, u32[]{:S(2)}) collective-permute-start(s32[2,512]{1,0:T(2,128)S(1)} %add_select_fusion), channel_id=1, source_target_pairs={{0,24},{8,16},{16,8},{24,0},{1,25},{9,17},{17,9},{25,1},{2,26},{10... | collective-permute-start | bytes 12296 | tf_op jit(solution)/shard_map/ppermute | solution.py:211
  7.2 24.7 %collective-permute-start.14 = (s32[2,512]{1,0:T(2,128)S(1)}, s32[2,512]{1,0:T(2,128)S(1)}, u32[]{:S(2)}, u32[]{:S(2)}) collective-permute-start(s32[2,512]{1,0:T(2,128)S(1)} %add_select_fusion), channel_id=1, source_target_pairs={{0,16},{8,24},{16,0},{24,8},{1,17},{9,25},{17,1},{25,9},{2,18},{10... | collective-permute-start | bytes 12296 | tf_op jit(solution)/shard_map/ppermute | solution.py:211
  7.2 25.1 %collective-permute-start.13 = (s32[2,512]{1,0:T(2,128)S(1)}, s32[2,512]{1,0:T(2,128)S(1)}, u32[]{:S(2)}, u32[]{:S(2)}) collective-permute-start(s32[2,512]{1,0:T(2,128)S(1)} %add_select_fusion), channel_id=1, source_target_pairs={{0,8},{8,0},{16,24},{24,16},{1,9},{9,1},{17,25},{25,17},{2,10},{10... | collective-permute-start | bytes 12296 | tf_op jit(solution)/shard_map/ppermute | solution.py:211
  13.4 36.4 %collective-permute-start.2 = (bf16[392,384]{1,0:T(8,128)(2,1)S(1)}, bf16[392,384]{1,0:T(8,128)(2,1)}, u32[]{:S(2)}, u32[]{:S(2)}) collective-permute-start(bf16[392,384]{1,0:T(8,128)(2,1)S(1)} %get-tuple-element.215), channel_id=1, source_target_pairs={{0,4},{2,6},{4,0},{6,2},{1,5},{3,7},{5,1},{7,3},{8,12},{10,14},{12... | collective-permute-start | bytes 903176 | tf_op jit(solution)/shard_map/ppermute | solution.py:211
  15.1 27.8 %collective-permute-start = (bf16[392,384]{1,0:T(8,128)(2,1)S(1)}, bf16[392,384]{1,0:T(8,128)(2,1)}, u32[]{:S(2)}, u32[]{:S(2)}) collective-permute-start(bf16[392,384]{1,0:T(8,128)(2,1)S(1)} %get-tuple-element.215), channel_id=1, source_target_pairs={{0,2},{2,0},{4,6},{6,4},{1,3},{3,1},{5,7},{7,5},{8,10},{10,8},{12,... | collective-permute-start | bytes 903176 | tf_op jit(solution)/shard_map/ppermute | solution.py:211
  32.2 23.7 %collective-permute-start.26 = (bf16[256,768]{1,0:T(8,128)(2,1)}, bf16[256,768]{1,0:T(8,128)(2,1)}, u32[]{:S(2)}, u32[]{:S(2)}) collective-permute-start(bf16[256,768]{1,0:T(8,128)(2,1)} %slice.847), channel_id=1, source_target_pairs={{0,24},{8,16},{16,8},{24,0},{1,25},{9,17},{17,9},{25,1},{2,26},{10... | collective-permute-start | bytes 1179656 | tf_op jit(solution)/shard_map/ppermute | solution.py:211
  39.3 28.5 %collective-permute-start.24 = (bf16[256,768]{1,0:T(8,128)(2,1)}, bf16[256,768]{1,0:T(8,128)(2,1)}, u32[]{:S(2)}, u32[]{:S(2)}) collective-permute-start(bf16[256,768]{1,0:T(8,128)(2,1)} %slice.847), channel_id=1, source_target_pairs={{0,16},{8,24},{16,0},{24,8},{1,17},{9,25},{17,1},{25,9},{2,18},{10... | collective-permute-start | bytes 1179656 | tf_op jit(solution)/shard_map/ppermute | solution.py:211
  42.9 25.0 %collective-permute-start.22 = (bf16[256,768]{1,0:T(8,128)(2,1)}, bf16[256,768]{1,0:T(8,128)(2,1)}, u32[]{:S(2)}, u32[]{:S(2)}) collective-permute-start(bf16[256,768]{1,0:T(8,128)(2,1)} %slice.847), channel_id=1, source_target_pairs={{0,8},{8,0},{16,24},{24,16},{1,9},{9,1},{17,25},{25,17},{2,10},{10... | collective-permute-start | bytes 1179656 | tf_op jit(solution)/shard_map/ppermute | solution.py:211
  44.6 23.8 %collective-permute-start.4 = (bf16[392,384]{1,0:T(8,128)(2,1)}, bf16[392,384]{1,0:T(8,128)(2,1)}, u32[]{:S(2)}, u32[]{:S(2)}) collective-permute-start(bf16[392,384]{1,0:T(8,128)(2,1)} %collective-permute-done), channel_id=1, source_target_pairs={{0,4},{2,6},{4,0},{6,2},{1,5},{3,7},{5,1},{7,3},{8,12},{10,14},{12... | collective-permute-start | bytes 903176 | tf_op jit(solution)/shard_map/ppermute | solution.py:211
  107.7 30.0 %collective-permute-start.29 = (bf16[2,192,1536]{2,1,0:T(8,128)(2,1)}, bf16[2,192,1536]{2,1,0:T(8,128)(2,1)}, u32[]{:S(2)}, u32[]{:S(2)}) collective-permute-start(bf16[2,192,1536]{2,1,0:T(8,128)(2,1)} %get-tuple-element.139), channel_id=1, source_target_pairs={{0,4},{2,6},{4,0},{6,2},{1,5},{3,7},{5,1},{7,3},{8,12},{10,14},{12... | collective-permute-start | bytes 3538952 | tf_op jit(solution)/shard_map/ppermute | solution.py:211
  109.2 31.4 %collective-permute-start.28 = (bf16[2,192,1536]{2,1,0:T(8,128)(2,1)}, bf16[2,192,1536]{2,1,0:T(8,128)(2,1)}, u32[]{:S(2)}, u32[]{:S(2)}) collective-permute-start(bf16[2,192,1536]{2,1,0:T(8,128)(2,1)} %get-tuple-element.139), channel_id=1, source_target_pairs={{0,2},{2,0},{4,6},{6,4},{1,3},{3,1},{5,7},{7,5},{8,10},{10,8},{12,... | collective-permute-start | bytes 3538952 | tf_op jit(solution)/shard_map/ppermute | solution.py:211
  136.4 29.6 %collective-permute-start.32 = (bf16[2,192,1536]{2,1,0:T(8,128)(2,1)S(1)}, bf16[2,192,1536]{2,1,0:T(8,128)(2,1)S(1)}, u32[]{:S(2)}, u32[]{:S(2)}) collective-permute-start(bf16[2,192,1536]{2,1,0:T(8,128)(2,1)S(1)} %copy-done.23), channel_id=1, source_target_pairs={{0,4},{2,6},{4,0},{6,2},{1,5},{3,7},{5,1},{7,3},{8,12},{10,14},{12... | collective-permute-start | bytes 3538952 | tf_op jit(solution)/shard_map/ppermute | solution.py:211
  137.0 28.9 %collective-permute-start.31 = (bf16[2,192,1536]{2,1,0:T(8,128)(2,1)S(1)}, bf16[2,192,1536]{2,1,0:T(8,128)(2,1)S(1)}, u32[]{:S(2)}, u32[]{:S(2)}) collective-permute-start(bf16[2,192,1536]{2,1,0:T(8,128)(2,1)S(1)} %copy-done.23), channel_id=1, source_target_pairs={{0,2},{2,0},{4,6},{6,4},{1,3},{3,1},{5,7},{7,5},{8,10},{10,8},{12,... | collective-permute-start | bytes 3538952 | tf_op jit(solution)/shard_map/ppermute | solution.py:211
  137.7 59.1 %collective-permute-start.30 = (bf16[2,192,1536]{2,1,0:T(8,128)(2,1)}, bf16[2,192,1536]{2,1,0:T(8,128)(2,1)S(1)}, u32[]{:S(2)}, u32[]{:S(2)}) collective-permute-start(bf16[2,192,1536]{2,1,0:T(8,128)(2,1)} %collective-permute-done.29), channel_id=1, source_target_pairs={{0,2},{2,0},{4,6},{6,4},{1,3},{3,1},{5,7},{7,5},{8,10},{10,8},{12,... | collective-permute-start | bytes 3538952 | tf_op jit(solution)/shard_map/ppermute | solution.py:211
  143.0 24.6 %collective-permute-start.20 = (bf16[256,768]{1,0:T(8,128)(2,1)S(1)}, bf16[256,768]{1,0:T(8,128)(2,1)S(1)}, u32[]{:S(2)}, u32[]{:S(2)}) collective-permute-start(bf16[256,768]{1,0:T(8,128)(2,1)S(1)} %slice.842), channel_id=1, source_target_pairs={{0,24},{8,16},{16,8},{24,0},{1,25},{9,17},{17,9},{25,1},{2,26},{10... | collective-permute-start | bytes 1179656 | tf_op jit(solution)/shard_map/ppermute | solution.py:211
  145.4 31.8 %collective-permute-start.18 = (bf16[256,768]{1,0:T(8,128)(2,1)S(1)}, bf16[256,768]{1,0:T(8,128)(2,1)S(1)}, u32[]{:S(2)}, u32[]{:S(2)}) collective-permute-start(bf16[256,768]{1,0:T(8,128)(2,1)S(1)} %slice.842), channel_id=1, source_target_pairs={{0,16},{8,24},{16,0},{24,8},{1,17},{9,25},{17,1},{25,9},{2,18},{10... | collective-permute-start | bytes 1179656 | tf_op jit(solution)/shard_map/ppermute | solution.py:211
  166.0 25.6 %collective-permute-start.33 = (bf16[2,192,1536]{2,1,0:T(8,128)(2,1)S(1)}, bf16[2,192,1536]{2,1,0:T(8,128)(2,1)S(1)}, u32[]{:S(2)}, u32[]{:S(2)}) collective-permute-start(bf16[2,192,1536]{2,1,0:T(8,128)(2,1)S(1)} %collective-permute-done.31), channel_id=1, source_target_pairs={{0,4},{2,6},{4,0},{6,2},{1,5},{3,7},{5,1},{7,3},{8,12},{10,14},{12... | collective-permute-start | bytes 3538952 | tf_op jit(solution)/shard_map/ppermute | solution.py:211
  266.6 46.6 %collective-permute-start.55 = (bf16[192,1536]{1,0:T(8,128)(2,1)S(1)}, bf16[192,1536]{1,0:T(8,128)(2,1)S(1)}, u32[]{:S(2)}, u32[]{:S(2)}) collective-permute-start(bf16[192,1536]{1,0:T(8,128)(2,1)S(1)} %slice.907), channel_id=1, source_target_pairs={{0,4},{2,6},{4,0},{6,2},{1,5},{3,7},{5,1},{7,3},{8,12},{10,14},{12... | collective-permute-start | bytes 1769480 | tf_op jit(solution)/shard_map/ppermute | solution.py:211
  273.6 46.9 %collective-permute-start.53 = (bf16[192,1536]{1,0:T(8,128)(2,1)S(1)}, bf16[192,1536]{1,0:T(8,128)(2,1)S(1)}, u32[]{:S(2)}, u32[]{:S(2)}) collective-permute-start(bf16[192,1536]{1,0:T(8,128)(2,1)S(1)} %get-tuple-element.129), channel_id=1, source_target_pairs={{0,4},{2,6},{4,0},{6,2},{1,5},{3,7},{5,1},{7,3},{8,12},{10,14},{12... | collective-permute-start | bytes 1769480 | tf_op jit(solution)/shard_map/ppermute | solution.py:211
  285.3 27.1 %collective-permute-start.36 = (bf16[256,768]{1,0:T(8,128)(2,1)S(1)}, bf16[256,768]{1,0:T(8,128)(2,1)S(1)}, u32[]{:S(2)}, u32[]{:S(2)}) collective-permute-start(bf16[256,768]{1,0:T(8,128)(2,1)S(1)} %get-tuple-element.164), channel_id=1, source_target_pairs={{0,16},{8,24},{16,0},{24,8},{1,17},{9,25},{17,1},{25,9},{2,18},{10... | collective-permute-start | bytes 1179656 | tf_op jit(solution)/shard_map/ppermute | solution.py:211
  289.2 32.0 %collective-permute-start.51 = (bf16[192,1536]{1,0:T(8,128)(2,1)S(1)}, bf16[192,1536]{1,0:T(8,128)(2,1)S(1)}, u32[]{:S(2)}, u32[]{:S(2)}) collective-permute-start(bf16[192,1536]{1,0:T(8,128)(2,1)S(1)} %get-tuple-element.130), channel_id=1, source_target_pairs={{0,2},{2,0},{4,6},{6,4},{1,3},{3,1},{5,7},{7,5},{8,10},{10,8},{12,... | collective-permute-start | bytes 1769480 | tf_op jit(solution)/shard_map/ppermute | solution.py:211
  298.5 24.1 %collective-permute-start.50 = (bf16[192,1536]{1,0:T(8,128)(2,1)S(1)}, bf16[192,1536]{1,0:T(8,128)(2,1)S(1)}, u32[]{:S(2)}, u32[]{:S(2)}) collective-permute-start(bf16[192,1536]{1,0:T(8,128)(2,1)S(1)} %get-tuple-element.132), channel_id=1, source_target_pairs={{0,2},{2,0},{4,6},{6,4},{1,3},{3,1},{5,7},{7,5},{8,10},{10,8},{12,... | collective-permute-start | bytes 1769480 | tf_op jit(solution)/shard_map/ppermute | solution.py:211
  312.5 42.1 %collective-permute-start.48 = (bf16[192,1536]{1,0:T(8,128)(2,1)S(1)}, bf16[192,1536]{1,0:T(8,128)(2,1)S(1)}, u32[]{:S(2)}, u32[]{:S(2)}) collective-permute-start(bf16[192,1536]{1,0:T(8,128)(2,1)S(1)} %get-tuple-element.133), channel_id=1, source_target_pairs={{0,4},{2,6},{4,0},{6,2},{1,5},{3,7},{5,1},{7,3},{8,12},{10,14},{12... | collective-permute-start | bytes 1769480 | tf_op jit(solution)/shard_map/ppermute | solution.py:211
  315.9 38.8 %collective-permute-start.59 = (bf16[192,1536]{1,0:T(8,128)(2,1)S(1)}, bf16[192,1536]{1,0:T(8,128)(2,1)S(1)}, u32[]{:S(2)}, u32[]{:S(2)}) collective-permute-start(bf16[192,1536]{1,0:T(8,128)(2,1)S(1)} %get-tuple-element.123), channel_id=1, source_target_pairs={{0,4},{2,6},{4,0},{6,2},{1,5},{3,7},{5,1},{7,3},{8,12},{10,14},{12... | collective-permute-start | bytes 1769480 | tf_op jit(solution)/shard_map/ppermute | solution.py:211
  320.6 34.1 %collective-permute-start.57 = (bf16[192,1536]{1,0:T(8,128)(2,1)S(1)}, bf16[192,1536]{1,0:T(8,128)(2,1)S(1)}, u32[]{:S(2)}, u32[]{:S(2)}) collective-permute-start(bf16[192,1536]{1,0:T(8,128)(2,1)S(1)} %get-tuple-element.124), channel_id=1, source_target_pairs={{0,2},{2,0},{4,6},{6,4},{1,3},{3,1},{5,7},{7,5},{8,10},{10,8},{12,... | collective-permute-start | bytes 1769480 | tf_op jit(solution)/shard_map/ppermute | solution.py:211
  321.2 33.5 %collective-permute-start.56 = (bf16[192,1536]{1,0:T(8,128)(2,1)S(1)}, bf16[192,1536]{1,0:T(8,128)(2,1)S(1)}, u32[]{:S(2)}, u32[]{:S(2)}) collective-permute-start(bf16[192,1536]{1,0:T(8,128)(2,1)S(1)} %get-tuple-element.126), channel_id=1, source_target_pairs={{0,2},{2,0},{4,6},{6,4},{1,3},{3,1},{5,7},{7,5},{8,10},{10,8},{12,... | collective-permute-start | bytes 1769480 | tf_op jit(solution)/shard_map/ppermute | solution.py:211
  322.6 32.1 %collective-permute-start.54 = (bf16[192,1536]{1,0:T(8,128)(2,1)S(1)}, bf16[192,1536]{1,0:T(8,128)(2,1)S(1)}, u32[]{:S(2)}, u32[]{:S(2)}) collective-permute-start(bf16[192,1536]{1,0:T(8,128)(2,1)S(1)} %get-tuple-element.127), channel_id=1, source_target_pairs={{0,4},{2,6},{4,0},{6,2},{1,5},{3,7},{5,1},{7,3},{8,12},{10,14},{12... | collective-permute-start | bytes 1769480 | tf_op jit(solution)/shard_map/ppermute | solution.py:211
  354.6 26.5 %collective-permute-start.38 = (bf16[4,256,768]{2,1,0:T(8,128)(2,1)}, bf16[4,256,768]{2,1,0:T(8,128)(2,1)}, u32[]{:S(2)}, u32[]{:S(2)}) collective-permute-start(bf16[4,256,768]{2,1,0:T(8,128)(2,1)} %convolution_convert_fusion.4), channel_id=1, source_target_pairs={{0,1},{1,0},{2,3},{3,2},{4,5},{5,4},{6,7},{7,6},{8,9},{9,8},{10,11... | collective-permute-start | bytes 4718600 | tf_op jit(solution)/shard_map/ppermute | solution.py:211
  355.8 28.0 %collective-permute-start.60 = (bf16[1,512,384]{2,1,0:T(8,128)(2,1)}, bf16[1,512,384]{2,1,0:T(8,128)(2,1)}, u32[]{:S(2)}, u32[]{:S(2)}) collective-permute-start(bf16[1,512,384]{2,1,0:T(8,128)(2,1)} %get-tuple-element.155), channel_id=1, source_target_pairs={{0,4},{2,6},{4,0},{6,2},{1,5},{3,7},{5,1},{7,3},{8,12},{10,14},{12... | collective-permute-start | bytes 1179656 | tf_op jit(solution)/shard_map/ppermute | solution.py:211
  358.8 30.2 %collective-permute-start.63 = (bf16[1,512,384]{2,1,0:T(8,128)(2,1)}, bf16[1,512,384]{2,1,0:T(8,128)(2,1)}, u32[]{:S(2)}, u32[]{:S(2)}) collective-permute-start(bf16[1,512,384]{2,1,0:T(8,128)(2,1)} %get-tuple-element.157), channel_id=1, source_target_pairs={{0,2},{2,0},{4,6},{6,4},{1,3},{3,1},{5,7},{7,5},{8,10},{10,8},{12,... | collective-permute-start | bytes 1179656 | tf_op jit(solution)/shard_map/ppermute | solution.py:211
  387.8 32.1 %collective-permute-start.40 = (bf16[256,768]{1,0:T(8,128)(2,1)S(1)}, bf16[256,768]{1,0:T(8,128)(2,1)S(1)}, u32[]{:S(2)}, u32[]{:S(2)}) collective-permute-start(bf16[256,768]{1,0:T(8,128)(2,1)S(1)} %get-tuple-element.161), channel_id=1, source_target_pairs={{0,16},{8,24},{16,0},{24,8},{1,17},{9,25},{17,1},{25,9},{2,18},{10... | collective-permute-start | bytes 1179656 | tf_op jit(solution)/shard_map/ppermute | solution.py:211
  428.5 24.3 %collective-permute-start.66 = (f32[512,768]{1,0:T(8,128)}, f32[512,768]{1,0:T(8,128)}, u32[]{:S(2)}, u32[]{:S(2)}) collective-permute-start(f32[512,768]{1,0:T(8,128)} %convolution_bitcast_fusion), channel_id=1, source_target_pairs={{0,1},{1,0},{2,3},{3,2},{4,5},{5,4},{6,7},{7,6},{8,9},{9,8},{10,11... | collective-permute-start | bytes 4718600 | tf_op jit(solution)/shard_map/ppermute | solution.py:211
  (133 other events, 1481.2 us)
